TPU v7x, 256 devices: a whole 4x4x8 slice. The times are simulated.
256 devices in a mesh: blk: 8 (over y_hi, x), sec: 32 (over y_lo, z, core).
Axes of the slice: x: 4, y: 4 (y_hi: 2, y_lo: 2; y = y_hi * 2 + y_lo), z: 8, core: 2. Of those that a mesh axis runs over, the one named last changes fastest.
Arguments:
- wavefunction: float32 [16, 256, 256], P('blk', 'sec'), may hold values from -6 to 6
- sector_sizes: int32 [16, 2], replicated, may hold values from 128 to 256, as said below
- env_left: float32 [8, 32, 8, 3, 256, 256], P('blk', 'sec'), may hold values from -0.375 to 0.375
- env_right: float32 [8, 32, 8, 3, 256, 256], P('blk', 'sec'), may hold values from -0.375 to 0.375
- mpo_weight: float32 [26], replicated, may hold values from -0.4 to 0.4
- bond_index: int32 [8, 32, 8, 3], P('blk', 'sec'), may hold values from 0 to 25
- in_pair: int32 [8, 32, 8, 3], P('blk', 'sec'), may hold values from 0 to 1
- out_pair: int32 [8, 32, 8, 3], P('blk', 'sec'), may hold values from -1 to 1
Outputs:
- applied: float32 [16, 256, 256], P('blk', 'sec')
Inputs may be any that keep to these rules, and one draw needn't show every extreme that they name: `sector_sizes`: row p holds the left and right states of pair p; some pair has 256 of each and another has 128 of each. `out_pair`: -1 marks an empty slot.
All inputs are finite; a program needn't handle non-finite values.
Results may differ from a plain program's by a relative error of at most 0.0001.
Values sent between devices are 32-bit elements; how exact they have to be, the bound alone decides.
No kernel may reach another device: no remote copies, remote signals or barrier semaphores. Data moves between devices by JAX's collectives and lax.ppermute only.
A program may use at most 128 MiB of HBM per device.

v0:
```python
import jax
import jax.numpy as jnp
from jax import lax
from jax.sharding import PartitionSpec as P


def from_behind(value, axis, steps):
    count = lax.axis_size(axis)
    pairs = [(source, (source + steps) % count) for source in range(count)]
    return lax.ppermute(value, axis, pairs)


def cycle_steps(panel_block, groups, my_group, step_ahead, step_back):
    result = [(panel_block, my_group)]
    forward_panel = panel_block
    backward_panel = panel_block
    for offset in range(1, groups // 2 + 1):
        forward_panel = step_ahead(forward_panel)
        result.append((forward_panel, (my_group - offset) % groups))
    for offset in range(1, (groups - 1) // 2 + 1):
        backward_panel = step_back(backward_panel)
        result.append((backward_panel, (my_group + offset) % groups))
    return result


def contract_rows(panel_block, left_slots, in_slots, source):
    env_block = lax.dynamic_index_in_dim(left_slots, source, 0, keepdims=False)
    chosen_pairs = lax.dynamic_index_in_dim(in_slots, source, 0, keepdims=False)
    chosen = jnp.take(lax.all_gather(panel_block, "sec", axis=1, tiled=True), chosen_pairs, axis=0)
    return jnp.einsum(
        "kxu,kus->kxs",
        env_block,
        chosen,
        precision=lax.Precision.HIGHEST,
        preferred_element_type=jnp.float32,
    )


def apply_right(partial_sums, product, right_slots, routing, source):
    env_block = lax.dynamic_index_in_dim(right_slots, source, 0, keepdims=False)
    term_value = jnp.einsum(
        "inr,ior->ino",
        product,
        env_block,
        precision=lax.Precision.HIGHEST,
        preferred_element_type=jnp.float32,
    )
    weights = lax.dynamic_index_in_dim(routing, source, 0, keepdims=False)
    return partial_sums + jnp.einsum(
        "tp,tad->pad",
        weights,
        term_value,
        precision=lax.Precision.HIGHEST,
        preferred_element_type=jnp.float32,
    )


def local(
    wavefunction, sector_sizes, env_left, env_right, mpo_weight, bond_index, in_pair, out_pair
):
    groups = lax.axis_size("blk")
    my_group = lax.axis_index("blk")
    my_owner = lax.axis_index("sec")
    pairs_here, row_count, states = wavefunction.shape
    group_sizes = lax.dynamic_slice_in_dim(sector_sizes, my_group * pairs_here, pairs_here, 0)
    row_ids = my_owner * row_count + jnp.arange(row_count, dtype=jnp.int32)
    col_ids = jnp.arange(states, dtype=jnp.int32)
    valid_mask = (
        (row_ids[None, :, None] < group_sizes[:, 0, None, None])
        & (col_ids[None, None, :] < group_sizes[:, 1, None, None])
    ).astype(jnp.float32)
    local_rows = wavefunction * valid_mask
    left_slots = env_left[0, 0]
    right_slots = env_right[0, 0]
    in_slots = in_pair[0, 0]
    bond_slots = bond_index[0, 0]
    live_slots = (out_pair[0, 0] >= 0).astype(jnp.float32)
    bond_ids = jnp.arange(mpo_weight.shape[0], dtype=jnp.int32)
    coupling = (
        jnp.sum(jnp.where(bond_slots[..., None] == bond_ids, mpo_weight, 0.0), axis=-1) * live_slots
    )
    pair_ids = jnp.arange(pairs_here, dtype=jnp.int32)
    routing = (out_pair[0, 0][..., None] == pair_ids).astype(jnp.float32) * coupling[..., None]
    partial_sums = jnp.zeros((pairs_here, states, states), jnp.float32)
    panels = cycle_steps(
        local_rows,
        groups,
        my_group,
        lambda moving: from_behind(moving, "blk", 1),
        lambda moving: from_behind(moving, "blk", -1),
    )
    for panel_block, source in panels:
        product = contract_rows(panel_block, left_slots, in_slots, source)
        partial_sums = apply_right(partial_sums, product, right_slots, routing, source)
    summed = lax.psum_scatter(partial_sums, "sec", scatter_dimension=1, tiled=True)
    return summed * valid_mask


def solution(mesh):
    return jax.shard_map(
        local,
        mesh=mesh,
        in_specs=(
            P("blk", "sec", None),
            P(),
            P("blk", "sec", None, None, None, None),
            P("blk", "sec", None, None, None, None),
            P(),
            P("blk", "sec", None, None),
            P("blk", "sec", None, None),
            P("blk", "sec", None, None),
        ),
        out_specs=P("blk", "sec", None),
        check_vma=False,
    )
```

profile of v0, /device:TPU:1, one launch (start us, length us, event | category | flops | bytes accessed | tf_op | source)
XLA Modules:
  0.0 590.3 jit_solution(10597719792938194536)
XLA Ops:
  6.5 0.7 copy-done
  7.5 0.8 and_select_fusion.1
  8.2 2.1 collective-permute-start
  10.4 4.0 collective-permute-start.4
  14.4 39.6 %all_gather.24 = f32[2,256,256]{2,0,1:T(2,128)S(1)} all-gather(f32[2,8,256]{2,0,1:T(2,128)S(1)} %and_select_fusion.1), channel_id=1, replica_groups=mesh['blk'=8,'sec'=32] {'sec'}, dimensions={1}, use_global_device_ids=true | all-gather | bytes 540672 | tf_op jit(solution)/shard_map/all_gather | solution.py:29
  53.9 1.6 fusion.104
  55.7 0.7 copy.91
  56.4 0.7 copy.92
  57.1 0.8 select_reduce_fusion
  57.9 0.7 compare_select_fusion.9
  59.4 2.1 fusion.39
  61.6 2.0 fusion.37
  63.6 2.2 fusion.7
  65.8 32.1 %all_gather.25 = f32[2,256,256]{2,0,1:T(2,128)S(1)} all-gather(f32[2,8,256]{2,0,1:T(2,128)S(1)} %collective-permute-done), channel_id=1, replica_groups=mesh['blk'=8,'sec'=32] {'sec'}, dimensions={1}, use_global_device_ids=true | all-gather | bytes 540672 | tf_op jit(solution)/shard_map/all_gather | solution.py:29
  98.6 2.1 fusion.35
  100.7 2.0 fusion.33
  102.8 33.9 %all_gather.29 = f32[2,256,256]{2,0,1:T(2,128)S(1)} all-gather(f32[2,8,256]{2,0,1:T(2,128)S(1)} %collective-permute-done.4), channel_id=1, replica_groups=mesh['blk'=8,'sec'=32] {'sec'}, dimensions={1}, use_global_device_ids=true | all-gather | bytes 540672 | tf_op jit(solution)/shard_map/all_gather | solution.py:29
  136.8 2.3 convolution_add_fusion.6
  139.7 2.1 fusion.19
  141.9 2.0 fusion.17
  143.9 5.1 collective-permute-start.5
  149.1 32.7 %all_gather.26 = f32[2,256,256]{2,0,1:T(2,128)S(1)} all-gather(f32[2,8,256]{2,0,1:T(2,128)S(1)} %collective-permute-done.1), channel_id=1, replica_groups=mesh['blk'=8,'sec'=32] {'sec'}, dimensions={1}, use_global_device_ids=true | all-gather | bytes 540672 | tf_op jit(solution)/shard_map/all_gather | solution.py:29
  182.4 2.1 fusion.31
  184.5 2.0 fusion.29
  186.6 33.6 %all_gather.30 = f32[2,256,256]{2,0,1:T(2,128)S(1)} all-gather(f32[2,8,256]{2,0,1:T(2,128)S(1)} %collective-permute-done.5), channel_id=1, replica_groups=mesh['blk'=8,'sec'=32] {'sec'}, dimensions={1}, use_global_device_ids=true | all-gather | bytes 540672 | tf_op jit(solution)/shard_map/all_gather | solution.py:29
  220.2 2.3 convolution_add_fusion.5
  223.1 2.1 fusion.15
  225.4 2.0 fusion.13
  227.4 5.1 collective-permute-start.6
  232.6 32.7 %all_gather.27 = f32[2,256,256]{2,0,1:T(2,128)S(1)} all-gather(f32[2,8,256]{2,0,1:T(2,128)S(1)} %collective-permute-done.2), channel_id=1, replica_groups=mesh['blk'=8,'sec'=32] {'sec'}, dimensions={1}, use_global_device_ids=true | all-gather | bytes 540672 | tf_op jit(solution)/shard_map/all_gather | solution.py:29
  265.9 2.1 fusion.27
  268.0 2.0 fusion.25
  270.1 33.5 %all_gather.31 = f32[2,256,256]{2,0,1:T(2,128)S(1)} all-gather(f32[2,8,256]{2,0,1:T(2,128)S(1)} %collective-permute-done.6), channel_id=1, replica_groups=mesh['blk'=8,'sec'=32] {'sec'}, dimensions={1}, use_global_device_ids=true | all-gather | bytes 540672 | tf_op jit(solution)/shard_map/all_gather | solution.py:29
  303.6 3.1 convolution_add_fusion.4
  307.3 2.2 fusion.11
  309.5 2.0 fusion.9
  311.6 4.1 collective-permute-done.3
  315.7 33.5 %all_gather.28 = f32[2,256,256]{2,0,1:T(2,128)S(1)} all-gather(f32[2,8,256]{2,0,1:T(2,128)S(1)} %collective-permute-done.3), channel_id=1, replica_groups=mesh['blk'=8,'sec'=32] {'sec'}, dimensions={1}, use_global_device_ids=true | all-gather | bytes 540672 | tf_op jit(solution)/shard_map/all_gather | solution.py:29
  349.2 1.5 gather_fusion.4
  350.7 2.4 fusion.23
  353.1 2.0 fusion.21
  355.1 2.3 convolution_add_fusion.3
  357.4 2.3 convolution_add_fusion.2
  359.7 2.3 convolution_add_fusion.1
  362.0 3.1 convolution_add_fusion
  366.4 215.4 %all-reduce.3.cloned.1.call-done = f32[2,256,256]{2,0,1:T(2,128)} async-done(((f32[2,256,256]{2,0,1:T(2,128)}), f32[2,256,256]{2,0,1:T(2,128)}) %all-reduce.3.cloned.1.call-update) | async-done | bytes 524304
  581.8 0.8 and_select_fusion
  582.6 0.6 copy.67
  (64 shorter events, 5.9 us)
Async XLA Ops:
  6.5 0.7 copy-start
  6.5 575.2 %all-reduce.3.cloned.1.call-start = ((), (), s32[]{:S(2)}) async-start(), calls=%async_computation | async-start | bytes 1048576
  8.2 57.6 %collective-permute-start = (f32[2,8,256]{2,0,1:T(2,128)S(1)}, f32[2,8,256]{2,0,1:T(2,128)S(1)}, u32[]{:S(2)}, u32[]{:S(2)}) collective-permute-start(f32[2,8,256]{2,0,1:T(2,128)S(1)} %and_select_fusion.1), channel_id=1, source_target_pairs={{0,32},{32,64},{64,96},{96,128},{128,160},{160,192},{192,224},{224... | collective-permute-start | bytes 49160 | tf_op jit(solution)/shard_map/ppermute | solution.py:10
  10.4 92.4 %collective-permute-start.4 = (f32[2,8,256]{2,0,1:T(2,128)S(1)}, f32[2,8,256]{2,0,1:T(2,128)S(1)}, u32[]{:S(2)}, u32[]{:S(2)}) collective-permute-start(f32[2,8,256]{2,0,1:T(2,128)S(1)} %and_select_fusion.1), channel_id=1, source_target_pairs={{0,224},{32,0},{64,32},{96,64},{128,96},{160,128},{192,160},{224,1... | collective-permute-start | bytes 49160 | tf_op jit(solution)/shard_map/ppermute | solution.py:10
  141.8 7.3 %collective-permute-start.1 = (f32[2,8,256]{2,0,1:T(2,128)S(1)}, f32[2,8,256]{2,0,1:T(2,128)S(1)}, u32[]{:S(2)}, u32[]{:S(2)}) collective-permute-start(f32[2,8,256]{2,0,1:T(2,128)S(1)} %collective-permute-done), channel_id=1, source_target_pairs={{0,32},{32,64},{64,96},{96,128},{128,160},{160,192},{192,224},{224... | collective-permute-start | bytes 49160 | tf_op jit(solution)/shard_map/ppermute | solution.py:10
  143.9 42.6 %collective-permute-start.5 = (f32[2,8,256]{2,0,1:T(2,128)S(1)}, f32[2,8,256]{2,0,1:T(2,128)S(1)}, u32[]{:S(2)}, u32[]{:S(2)}) collective-permute-start(f32[2,8,256]{2,0,1:T(2,128)S(1)} %collective-permute-done.4), channel_id=1, source_target_pairs={{0,224},{32,0},{64,32},{96,64},{128,96},{160,128},{192,160},{224,1... | collective-permute-start | bytes 49160 | tf_op jit(solution)/shard_map/ppermute | solution.py:10
  225.3 7.3 %collective-permute-start.2 = (f32[2,8,256]{2,0,1:T(2,128)S(1)}, f32[2,8,256]{2,0,1:T(2,128)S(1)}, u32[]{:S(2)}, u32[]{:S(2)}) collective-permute-start(f32[2,8,256]{2,0,1:T(2,128)S(1)} %collective-permute-done.1), channel_id=1, source_target_pairs={{0,32},{32,64},{64,96},{96,128},{128,160},{160,192},{192,224},{224... | collective-permute-start | bytes 49160 | tf_op jit(solution)/shard_map/ppermute | solution.py:10
  227.4 42.6 %collective-permute-start.6 = (f32[2,8,256]{2,0,1:T(2,128)S(1)}, f32[2,8,256]{2,0,1:T(2,128)S(1)}, u32[]{:S(2)}, u32[]{:S(2)}) collective-permute-start(f32[2,8,256]{2,0,1:T(2,128)S(1)} %collective-permute-done.5), channel_id=1, source_target_pairs={{0,224},{32,0},{64,32},{96,64},{128,96},{160,128},{192,160},{224,1... | collective-permute-start | bytes 49160 | tf_op jit(solution)/shard_map/ppermute | solution.py:10
  307.2 47.9 %copy-start.1 = (f32[2,256,256]{2,0,1:T(2,128)S(1)}, f32[2,256,256]{2,0,1:T(2,128)}, u32[]{:S(2)}) copy-start(f32[2,256,256]{2,0,1:T(2,128)} %convolution_add_fusion.4) | copy-start | bytes 1572868
  309.4 6.3 %collective-permute-start.3 = (f32[2,8,256]{2,0,1:T(2,128)S(1)}, f32[2,8,256]{2,0,1:T(2,128)S(1)}, u32[]{:S(2)}, u32[]{:S(2)}) collective-permute-start(f32[2,8,256]{2,0,1:T(2,128)S(1)} %collective-permute-done.2), channel_id=1, source_target_pairs={{0,32},{32,64},{64,96},{96,128},{128,160},{160,192},{192,224},{224... | collective-permute-start | bytes 49160 | tf_op jit(solution)/shard_map/ppermute | solution.py:10
  350.7 14.4 %copy-start.2 = (u32[256]{0:T(256)S(1)}, u32[256]{0:T(256)}, u32[]{:S(2)}) copy-start(u32[256]{0:T(256)} %constant.183) | copy-start | bytes 3076
Sparse Core Ops, SparseCore 0:
  365.2 216.4 all-reduce.2
where the time goes:
time: 598 us; the launch traced here: 590 us
  blocking collectives  271 us (45%)
  waiting for transfers between devices  220 us (37%)
  matrix products  53.4 us (9%)
  starting transfers between devices  16.6 us (3%)
  between operations  14.8 us (2%)
  local copies, waits for them, and re-layouts  11 us (2%)
    all_gather x8, blocking collectives, contract_rows(): lax.all_gather(panel_block, 'sec', axis=1, tiled=True)  271 us
    unnamed x2, waiting for transfers between devices  215 us
    dot_general x8, matrix products, apply_right(): jnp.einsum('tp,tad->pad', weights, term_value, precision=lax.Precision.HI...  19.8 us
    dot_general x8, matrix products, contract_rows(): jnp.einsum('kxu,kus->kxs', env_block, chosen, precision=lax.Precision.HIG...  17.3 us
    ppermute x7, starting transfers between devices, from_behind(): return lax.ppermute(value, axis, pairs)  16.6 us
    dot_general x8, matrix products, apply_right(): jnp.einsum('inr,ior->ino', product, env_block, precision=lax.Precision.HI...  16.4 us
  transfers between devices with their start and end apart: 8, of which 2 were waited for; matrix products, arithmetic and copies ran while one was open for 6% of the time, Pallas kernels for 0%

commit v1 on v0

v1 whole, which is shorter than its diff:
```python
import functools

import jax
import jax.numpy as jnp
from jax import lax
from jax.experimental import pallas as pl
from jax.experimental.pallas import tpu as pltpu
from jax.sharding import Mesh, PartitionSpec as P

GROUPS, PAIRS, SLOTS, STATES, ROWS = 8, 2, 3, 256, 8
RUNS = STATES // (2 * ROWS)
F32, BF16 = jnp.float32, jnp.bfloat16


def split(value):
    high = value.astype(BF16)
    return high, (value - high.astype(F32)).astype(BF16)


def dot3(left, right, contract):
    dot = functools.partial(
        lax.dot_general, dimension_numbers=(contract, ((), ())), preferred_element_type=F32
    )
    return dot(left[0], right[0]) + dot(left[0], right[1]) + dot(left[1], right[0])


def contract_kernel(
    place, sizes, weight, bond, in_pair, out_pair,
    x_same, x_other, left, right, keep, give, x_high, x_low, total,
):
    step = pl.program_id(0)
    core = place[0]
    source = place[1 + step]

    @pl.when(step == 0)
    def _():
        total[...] = jnp.zeros_like(total)

    row_ids = lax.broadcasted_iota(jnp.int32, (RUNS, 2, ROWS, STATES), 0) * (2 * ROWS)
    row_ids += lax.broadcasted_iota(jnp.int32, (RUNS, 2, ROWS, STATES), 1) * ROWS
    row_ids += lax.broadcasted_iota(jnp.int32, (RUNS, 2, ROWS, STATES), 2)
    row_ids = row_ids.reshape(STATES, STATES)
    col_ids = lax.broadcasted_iota(jnp.int32, (STATES, STATES), 1)
    for pair in range(PAIRS):
        same, other = x_same[0, :, pair], x_other[0, :, pair]
        first = jnp.where(core == 0, same, other)
        second = jnp.where(core == 0, other, same)
        whole = jnp.stack([first, second], axis=1).reshape(STATES, STATES)
        here = source * PAIRS + pair
        valid = (row_ids < sizes[here, 0]) & (col_ids < sizes[here, 1])
        x_high[pair], x_low[pair] = split(jnp.where(valid, whole, 0.0))

    for slot in range(SLOTS):
        target = out_pair[source, slot]

        @pl.when(target >= 0)
        def _():
            pair = in_pair[source, slot]
            inner = dot3(split(left[0, slot]), (x_high[pair], x_low[pair]), ((1,), (0,)))
            inner = inner * weight[bond[source, slot]]
            total[target] += dot3(split(inner), split(right[0, slot]), ((1,), (1,)))

    @pl.when(step == pl.num_programs(0) - 1)
    def _():
        for pair in range(PAIRS):
            rows = total[pair].reshape(RUNS, 2, ROWS, STATES)
            keep[:, pair] = jnp.where(core == 0, rows[:, 0], rows[:, 1])
            give[:, pair] = jnp.where(core == 0, rows[:, 1], rows[:, 0])


def contract(place, sizes, weight, bond, in_pair, out_pair, x_same, x_other, left, right):
    steps = x_same.shape[0]
    panel = pl.BlockSpec((1, RUNS, PAIRS, ROWS, STATES), lambda i, *_: (i, 0, 0, 0, 0))
    env = pl.BlockSpec((1, SLOTS, STATES, STATES), lambda i, place, *_: (place[1 + i], 0, 0, 0))
    out = pl.BlockSpec((RUNS, PAIRS, ROWS, STATES), lambda i, *_: (0, 0, 0, 0))
    shape = jax.ShapeDtypeStruct((RUNS, PAIRS, ROWS, STATES), F32)
    return pl.pallas_call(
        contract_kernel,
        grid_spec=pltpu.PrefetchScalarGridSpec(
            num_scalar_prefetch=6,
            grid=(steps,),
            in_specs=[panel, panel, env, env],
            out_specs=[out, out],
            scratch_shapes=[
                pltpu.VMEM((PAIRS, STATES, STATES), BF16),
                pltpu.VMEM((PAIRS, STATES, STATES), BF16),
                pltpu.VMEM((PAIRS, STATES, STATES), F32),
            ],
        ),
        out_shape=[shape, shape],
        compiler_params=pltpu.CompilerParams(vmem_limit_bytes=32 * 2**20),
    )(place, sizes, weight, bond, in_pair, out_pair, x_same, x_other, left, right)


def swap_core(value):
    return lax.ppermute(value, "core", [(0, 1), (1, 0)])


def local(
    wavefunction, sector_sizes, env_left, env_right, mpo_weight, bond_index, in_pair, out_pair
):
    core = lax.axis_index("core")
    my_y, my_x = lax.axis_index("y_hi"), lax.axis_index("x")
    runs = lax.all_to_all(
        jnp.broadcast_to(wavefunction[None], (RUNS,) + wavefunction.shape), ("y_lo", "z"), 0, 0
    )
    across = lax.ppermute(runs, "y_hi", [(0, 1), (1, 0)])
    pieces, sources = [runs, across], [my_y * 4 + my_x, (1 - my_y) * 4 + my_x]
    for step in (1, 3, 2):
        ring = [(x, (x + step) % 4) for x in range(4)]
        there = (my_x - step) % 4
        pieces += [lax.ppermute(runs, "x", ring), lax.ppermute(across, "x", ring)]
        sources += [my_y * 4 + there, (1 - my_y) * 4 + there]
    x_same = jnp.stack(pieces)
    x_other = swap_core(x_same)
    place = jnp.stack([core] + sources).astype(jnp.int32)
    keep, give = contract(
        place, sector_sizes, mpo_weight, bond_index[0, 0], in_pair[0, 0], out_pair[0, 0],
        x_same, x_other, env_left[0, 0], env_right[0, 0],
    )
    half = keep + swap_core(give)
    summed = lax.all_to_all(half, ("y_lo", "z"), 0, 0).sum(0)

    owner = (lax.axis_index("y_lo") * 8 + lax.axis_index("z")) * 2 + core
    group_sizes = lax.dynamic_slice_in_dim(
        sector_sizes, (my_y * 4 + my_x) * PAIRS, PAIRS, 0
    )
    row_ids = owner * ROWS + jnp.arange(ROWS, dtype=jnp.int32)
    col_ids = jnp.arange(STATES, dtype=jnp.int32)
    valid = (row_ids[None, :, None] < group_sizes[:, 0, None, None]) & (
        col_ids[None, None, :] < group_sizes[:, 1, None, None]
    )
    return jnp.where(valid, summed, 0.0)


def solution(mesh):
    fine = Mesh(mesh.devices.reshape(2, 4, 2, 8, 2), ("y_hi", "x", "y_lo", "z", "core"))
    blk, sec = ("y_hi", "x"), ("y_lo", "z", "core")
    return jax.shard_map(
        local,
        mesh=fine,
        in_specs=(
            P(blk, sec, None),
            P(),
            P(blk, sec, None, None, None, None),
            P(blk, sec, None, None, None, None),
            P(),
            P(blk, sec, None, None),
            P(blk, sec, None, None),
            P(blk, sec, None, None),
        ),
        out_specs=P(blk, sec, None),
        check_vma=False,
    )
```

time: 598 us -> 92.5 us (0.15); the launches traced: 590 us -> 91.2 us
  blocking collectives: 271 us -> 18.7 us
  waiting for transfers between devices: 220 us -> 28.9 us
  matrix products: 53.4 us -> 0 us
  between operations: 14.8 us -> 0.14 us
  Pallas kernels: 0 us -> 13.7 us
    all_gather x8 -> x0, blocking collectives: 271 us -> none  [contract_rows(): lax.all_gather(panel_block, 'sec', axis=1, tiled=True)]
    unnamed x2 -> x0, waiting for transfers between devices: 215 us -> none
    dot_general x24 -> x0, matrix products: 53.4 us -> none  [the longest x8 19.8 us: apply_right(): jnp.einsum('tp,tad->pad', weights, term_value, precision=lax.Precision.HI...]
    all_to_all x0 -> x1, blocking collectives: none -> 18.7 us  [local(): lax.all_to_all(jnp.broadcast_to(wavefunction[None], (RUNS,) + wavefunctio...]
    ppermute x7 -> x9, waiting for transfers between devices: 4.15 us -> 19.9 us  [the longest x6 15.3 us: local(): pieces += [lax.ppermute(runs, 'x', ring), lax.ppermute(across, 'x', ring)]]
    pallas_call x0 -> x1, Pallas kernels: none -> 13.7 us  [contract(): pl.pallas_call(contract_kernel, grid_spec=pltpu.PrefetchScalarGridSpec(nu...]
    all_to_all x0 -> x1, waiting for transfers between devices: none -> 8.97 us  [local(): summed = lax.all_to_all(half, ('y_lo', 'z'), 0, 0).sum(0)]
    ppermute x7 -> x9, starting transfers between devices: 16.6 us -> 17.1 us  [the longest x6 8.38 us: local(): pieces += [lax.ppermute(runs, 'x', ring), lax.ppermute(across, 'x', ring)]]
  transfers between devices with their start and end apart: 8 -> 10, of which waited for: 2 -> 5; matrix products, arithmetic and copies ran while one was open for 6% -> 1% of each run, Pallas kernels for 0% -> 0%
where the time goes in v1:
time: 92.5 us; the launch traced here: 91.2 us
  waiting for transfers between devices  28.9 us (31%)
  starting transfers between devices  21.3 us (23%)
  blocking collectives  18.7 us (20%)
  Pallas kernels  13.7 us (15%)
  local copies, waits for them, and re-layouts  6.96 us (8%)
  other arithmetic  1.58 us (2%)
    all_to_all x1, blocking collectives, local(): lax.all_to_all(jnp.broadcast_to(wavefunction[None], (RUNS,) + wavefunctio...  18.7 us
    ppermute x6, waiting for transfers between devices, local(): pieces += [lax.ppermute(runs, 'x', ring), lax.ppermute(across, 'x', ring)]  15.3 us
    pallas_call x1, Pallas kernels, contract(): pl.pallas_call(contract_kernel, grid_spec=pltpu.PrefetchScalarGridSpec(nu...  13.7 us
    all_to_all x1, waiting for transfers between devices, local(): summed = lax.all_to_all(half, ('y_lo', 'z'), 0, 0).sum(0)  8.97 us
    ppermute x6, starting transfers between devices, local(): pieces += [lax.ppermute(runs, 'x', ring), lax.ppermute(across, 'x', ring)]  8.38 us
    ppermute x2, starting transfers between devices, swap_core(): return lax.ppermute(value, 'core', [(0, 1), (1, 0)])  6.03 us
    unnamed x22, local copies, waits for them, and re-layouts  5.81 us
    ppermute x2, waiting for transfers between devices, swap_core(): return lax.ppermute(value, 'core', [(0, 1), (1, 0)])  4.58 us
  transfers between devices with their start and end apart: 10, of which 5 were waited for; matrix products, arithmetic and copies ran while one was open for 1% of the time, Pallas kernels for 0%

profile of v1, /device:TPU:1, one launch (start us, length us, event | category | flops | bytes accessed | tf_op | source)
XLA Modules:
  0.0 91.2 jit_solution(6285647981609576594)
XLA Ops:
  0.0 0.7 broadcast_in_dim.5
  0.7 18.7 %all_to_all.10 = f32[16,2,8,256]{3,2,1,0:T(8,128)S(1)} all-to-all(f32[16,2,8,256]{3,2,1,0:T(8,128)S(1)} %broadcast_in_dim.5), channel_id=1, replica_groups=mesh['y_hi'=2,'x'=4,'y_lo'=2,'z'=8,'core'=2] {'y_lo','z'}, dimensions={0} | all-to-all | bytes 524288 | tf_op jit(solution)/shard_map/all_to_all | solution.py:104
  19.4 0.0 copy-start.3
  19.4 0.0 copy-start.4
  19.4 0.0 copy-start.5
  19.4 0.0 copy-start.6
  19.4 0.0 copy-start.2
  19.4 2.7 %collective-permute-start = (f32[16,2,8,256]{3,2,1,0:T(8,128)S(1)}, f32[16,2,8,256]{3,2,1,0:T(8,128)S(1)}, u32[]{:S(2)}, u32[]{:S(2)}) collective-permute-start(f32[16,2,8,256]{3,2,1,0:T(8,128)S(1)} %all_to_all.10), channel_id=1, source_target_pairs={{0,128},{128,0},{1,129},{129,1},{2,130},{130,2},{3,131},{131,3},{4... | collective-permute-start | bytes 786440 | tf_op jit(solution)/shard_map/ppermute | solution.py:107
  22.1 1.2 %collective-permute-start.1 = (f32[16,2,8,256]{3,2,1,0:T(8,128)S(1)}, f32[16,2,8,256]{3,2,1,0:T(8,128)S(1)}, u32[]{:S(2)}, u32[]{:S(2)}) collective-permute-start(f32[16,2,8,256]{3,2,1,0:T(8,128)S(1)} %all_to_all.10), channel_id=1, source_target_pairs={{0,32},{32,64},{64,96},{96,0},{1,33},{33,65},{65,97},{97,1},{2,34}... | collective-permute-start | bytes 786440 | tf_op jit(solution)/shard_map/ppermute | solution.py:112
  23.4 1.5 %collective-permute-start.3 = (f32[16,2,8,256]{3,2,1,0:T(8,128)S(1)}, f32[16,2,8,256]{3,2,1,0:T(8,128)S(1)}, u32[]{:S(2)}, u32[]{:S(2)}) collective-permute-start(f32[16,2,8,256]{3,2,1,0:T(8,128)S(1)} %all_to_all.10), channel_id=1, source_target_pairs={{0,96},{32,0},{64,32},{96,64},{1,97},{33,1},{65,33},{97,65},{2,98}... | collective-permute-start | bytes 786440 | tf_op jit(solution)/shard_map/ppermute | solution.py:112
  24.9 1.5 %collective-permute-start.5 = (f32[16,2,8,256]{3,2,1,0:T(8,128)S(1)}, f32[16,2,8,256]{3,2,1,0:T(8,128)S(1)}, u32[]{:S(2)}, u32[]{:S(2)}) collective-permute-start(f32[16,2,8,256]{3,2,1,0:T(8,128)S(1)} %all_to_all.10), channel_id=1, source_target_pairs={{0,64},{32,96},{64,0},{96,32},{1,65},{33,97},{65,1},{97,33},{2,66}... | collective-permute-start | bytes 786440 | tf_op jit(solution)/shard_map/ppermute | solution.py:112
  26.4 0.0 collective-permute-done
  26.4 1.0 %collective-permute-start.2 = (f32[16,2,8,256]{3,2,1,0:T(8,128)S(1)}, f32[16,2,8,256]{3,2,1,0:T(8,128)S(1)}, u32[]{:S(2)}, u32[]{:S(2)}) collective-permute-start(f32[16,2,8,256]{3,2,1,0:T(8,128)S(1)} %collective-permute-done), channel_id=1, source_target_pairs={{0,32},{32,64},{64,96},{96,0},{1,33},{33,65},{65,97},{97,1},{2,34}... | collective-permute-start | bytes 786440 | tf_op jit(solution)/shard_map/ppermute | solution.py:112
  27.5 1.7 %collective-permute-start.4 = (f32[16,2,8,256]{3,2,1,0:T(8,128)S(1)}, f32[16,2,8,256]{3,2,1,0:T(8,128)S(1)}, u32[]{:S(2)}, u32[]{:S(2)}) collective-permute-start(f32[16,2,8,256]{3,2,1,0:T(8,128)S(1)} %collective-permute-done), channel_id=1, source_target_pairs={{0,96},{32,0},{64,32},{96,64},{1,97},{33,1},{65,33},{97,65},{2,98}... | collective-permute-start | bytes 786440 | tf_op jit(solution)/shard_map/ppermute | solution.py:112
  29.1 0.0 collective-permute-done.1
  29.2 1.4 %collective-permute-start.6 = (f32[16,2,8,256]{3,2,1,0:T(8,128)S(1)}, f32[16,2,8,256]{3,2,1,0:T(8,128)S(1)}, u32[]{:S(2)}, u32[]{:S(2)}) collective-permute-start(f32[16,2,8,256]{3,2,1,0:T(8,128)S(1)} %collective-permute-done), channel_id=1, source_target_pairs={{0,64},{32,96},{64,0},{96,32},{1,65},{33,97},{65,1},{97,33},{2,66}... | collective-permute-start | bytes 786440 | tf_op jit(solution)/shard_map/ppermute | solution.py:112
  30.6 11.1 %collective-permute-done.2 = f32[16,2,8,256]{3,2,1,0:T(8,128)S(1)} collective-permute-done((f32[16,2,8,256]{3,2,1,0:T(8,128)S(1)}, f32[16,2,8,256]{3,2,1,0:T(8,128)S(1)}, u32[]{:S(2)}, u32[]{:S(2)}) %collective-permute-start.2) | collective-permute-done | bytes 262176 | tf_op jit(solution)/shard_map/ppermute | solution.py:112
  41.7 0.0 collective-permute-done.3
  41.7 0.0 collective-permute-done.4
  41.8 0.0 collective-permute-done.5
  41.8 4.3 %collective-permute-done.6 = f32[16,2,8,256]{3,2,1,0:T(8,128)S(1)} collective-permute-done((f32[16,2,8,256]{3,2,1,0:T(8,128)S(1)}, f32[16,2,8,256]{3,2,1,0:T(8,128)S(1)}, u32[]{:S(2)}, u32[]{:S(2)}) %collective-permute-start.6) | collective-permute-done | bytes 262176 | tf_op jit(solution)/shard_map/ppermute | solution.py:112
  46.1 3.9 %collective-permute-start.7 = (f32[8,16,2,8,256]{4,3,2,1,0:T(8,128)S(1)}, f32[8,16,2,8,256]{4,3,2,1,0:T(8,128)}, u32[]{:S(2)}, u32[]{:S(2)}) collective-permute-start(f32[8,16,2,8,256]{4,3,2,1,0:T(8,128)S(1)} %bitcast_dynamic-update-slice_fusion.x_same), channel_id=1, source_target_pairs={{0,1},{1,0},{2,3},{3,2},{4,5},{5,4},{6,7},{7,6},{8,9},{9,8},{10,11... | collective-permute-start | bytes 6291464 | tf_op jit(solution)/shard_map/ppermute | solution.py:96
  50.0 0.0 copy-done.3
  50.0 0.1 copy.9.sizes
  50.1 0.0 copy-done.4
  50.1 0.1 copy.13
  50.2 0.0 copy-done.5
  50.2 0.1 copy.14
  50.3 0.0 copy-done.6
  50.3 0.1 copy.15
  50.4 0.1 stack.66.place
  50.4 3.5 %collective-permute-done.7.x_other = f32[8,16,2,8,256]{4,3,2,1,0:T(8,128)} collective-permute-done((f32[8,16,2,8,256]{4,3,2,1,0:T(8,128)S(1)}, f32[8,16,2,8,256]{4,3,2,1,0:T(8,128)}, u32[]{:S(2)}, u32[]{:S(2)}) %collective-permute-start.7) | collective-permute-done | bytes 2097184 | tf_op jit(solution)/shard_map/ppermute | solution.py:96
  53.9 0.0 copy-done.2
  53.9 0.0 copy-start
  53.9 2.8 %copy-done = f32[1,1,8,3,256,256]{5,4,3,2,1,0:T(8,128)S(1)} copy-done((f32[1,1,8,3,256,256]{5,4,3,2,1,0:T(8,128)S(1)}, f32[1,1,8,3,256,256]{5,4,3,2,1,0:T(8,128)}, u32[]{:S(2)}) %copy-start) | copy-done | bytes 6291480
  56.7 0.0 copy-start.1
  56.7 2.8 %copy-done.1 = f32[1,1,8,3,256,256]{5,4,3,2,1,0:T(8,128)S(1)} copy-done((f32[1,1,8,3,256,256]{5,4,3,2,1,0:T(8,128)S(1)}, f32[1,1,8,3,256,256]{5,4,3,2,1,0:T(8,128)}, u32[]{:S(2)}) %copy-start.1) | copy-done | bytes 6291480
  59.5 13.7 %shard_map.82 = (f32[16,2,8,256]{3,2,1,0:T(8,128)S(1)}, f32[16,2,8,256]{3,2,1,0:T(8,128)S(1)}) custom-call(s32[9]{0:T(128)S(1)} %stack.66.place, s32[16,2]{1,0:T(8,128)S(1)} %copy.9.sizes, f32[26]{0:T(128)S(1)} %copy-done.2, s32[8,3]{1,0:T(8,128)S(1)} %bitcast.36, s32[8,3]{1,0:T(8,128)S(1)} %bitcast.37, s32[8,3]{1,0:T(8,128)S(1)} %bitcast.38, ...), custom_call_target="tpu_custom_call" | custom-call | tf_op jit(solution)/shard_map/pallas_call | solution.py:77
  73.2 2.1 %collective-permute-start.8 = (f32[16,2,8,256]{3,2,1,0:T(8,128)S(1)}, f32[16,2,8,256]{3,2,1,0:T(8,128)S(1)}, u32[]{:S(2)}, u32[]{:S(2)}) collective-permute-start(f32[16,2,8,256]{3,2,1,0:T(8,128)S(1)} %get-tuple-element.8), channel_id=1, source_target_pairs={{0,1},{1,0},{2,3},{3,2},{4,5},{5,4},{6,7},{7,6},{8,9},{9,8},{10,11... | collective-permute-start | bytes 786440 | tf_op jit(solution)/shard_map/ppermute | solution.py:96
  75.3 0.1 constant_dynamic-slice_fusion
  75.4 1.1 %collective-permute-done.8 = f32[16,2,8,256]{3,2,1,0:T(8,128)S(1)} collective-permute-done((f32[16,2,8,256]{3,2,1,0:T(8,128)S(1)}, f32[16,2,8,256]{3,2,1,0:T(8,128)S(1)}, u32[]{:S(2)}, u32[]{:S(2)}) %collective-permute-start.8) | collective-permute-done | bytes 262176 | tf_op jit(solution)/shard_map/ppermute | solution.py:96
  76.4 0.7 add.76
  77.2 4.2 %all-to-all-start.1 = ((f32[16,2,8,256]{3,2,1,0:T(8,128)}), f32[16,2,8,256]{3,2,1,0:T(8,128)S(1)}, u32[]{:S(2)}, u32[]{:S(2)}) async-start(f32[16,2,8,256]{3,2,1,0:T(8,128)} %add.76), calls=%async_computation.1 | async-start | bytes 524288 | tf_op jit(solution)/shard_map/all_to_all | solution.py:122
  81.4 0.1 iota_compare_fusion
  81.5 0.1 broadcast_compare_fusion
  81.5 9.0 %all-to-all-done.1 = f32[16,2,8,256]{3,2,1,0:T(8,128)S(1)} async-done(((f32[16,2,8,256]{3,2,1,0:T(8,128)}), f32[16,2,8,256]{3,2,1,0:T(8,128)S(1)}, u32[]{:S(2)}, u32[]{:S(2)}) %all-to-all-start.1) | async-done | bytes 262176 | tf_op jit(solution)/shard_map/all_to_all | solution.py:122
  90.5 0.7 and_select_fusion
  (11 shorter events, 0.2 us)
Async XLA Ops:
  19.4 30.6 %copy-start.3 = (s32[16,2]{0,1:T(2,128)S(1)}, s32[16,2]{0,1:T(2,128)}, u32[]{:S(2)}) copy-start(s32[16,2]{0,1:T(2,128)} %param.9) | copy-start | bytes 388
  19.4 30.7 %copy-start.4 = (s32[1,1,8,3]{2,1,3,0:T(1,128)S(1)}, s32[1,1,8,3]{2,1,3,0:T(1,128)}, u32[]{:S(2)}) copy-start(s32[1,1,8,3]{2,1,3,0:T(1,128)} %param.13) | copy-start | bytes 292
  19.4 30.8 %copy-start.5 = (s32[1,1,8,3]{2,1,3,0:T(1,128)S(1)}, s32[1,1,8,3]{2,1,3,0:T(1,128)}, u32[]{:S(2)}) copy-start(s32[1,1,8,3]{2,1,3,0:T(1,128)} %param.14) | copy-start | bytes 292
  19.4 30.9 %copy-start.6 = (s32[1,1,8,3]{2,1,3,0:T(1,128)S(1)}, s32[1,1,8,3]{2,1,3,0:T(1,128)}, u32[]{:S(2)}) copy-start(s32[1,1,8,3]{2,1,3,0:T(1,128)} %param.15) | copy-start | bytes 292
  19.4 34.5 %copy-start.2 = (f32[26]{0:T(128)S(1)}, f32[26]{0:T(128)}, u32[]{:S(2)}) copy-start(f32[26]{0:T(128)} %weight.1) | copy-start | bytes 316
  19.4 7.0 %collective-permute-start = (f32[16,2,8,256]{3,2,1,0:T(8,128)S(1)}, f32[16,2,8,256]{3,2,1,0:T(8,128)S(1)}, u32[]{:S(2)}, u32[]{:S(2)}) collective-permute-start(f32[16,2,8,256]{3,2,1,0:T(8,128)S(1)} %all_to_all.10), channel_id=1, source_target_pairs={{0,128},{128,0},{1,129},{129,1},{2,130},{130,2},{3,131},{131,3},{4... | collective-permute-start | bytes 786440 | tf_op jit(solution)/shard_map/ppermute | solution.py:107
  22.1 7.0 %collective-permute-start.1 = (f32[16,2,8,256]{3,2,1,0:T(8,128)S(1)}, f32[16,2,8,256]{3,2,1,0:T(8,128)S(1)}, u32[]{:S(2)}, u32[]{:S(2)}) collective-permute-start(f32[16,2,8,256]{3,2,1,0:T(8,128)S(1)} %all_to_all.10), channel_id=1, source_target_pairs={{0,32},{32,64},{64,96},{96,0},{1,33},{33,65},{65,97},{97,1},{2,34}... | collective-permute-start | bytes 786440 | tf_op jit(solution)/shard_map/ppermute | solution.py:112
  23.4 18.3 %collective-permute-start.3 = (f32[16,2,8,256]{3,2,1,0:T(8,128)S(1)}, f32[16,2,8,256]{3,2,1,0:T(8,128)S(1)}, u32[]{:S(2)}, u32[]{:S(2)}) collective-permute-start(f32[16,2,8,256]{3,2,1,0:T(8,128)S(1)} %all_to_all.10), channel_id=1, source_target_pairs={{0,96},{32,0},{64,32},{96,64},{1,97},{33,1},{65,33},{97,65},{2,98}... | collective-permute-start | bytes 786440 | tf_op jit(solution)/shard_map/ppermute | solution.py:112
  24.9 16.9 %collective-permute-start.5 = (f32[16,2,8,256]{3,2,1,0:T(8,128)S(1)}, f32[16,2,8,256]{3,2,1,0:T(8,128)S(1)}, u32[]{:S(2)}, u32[]{:S(2)}) collective-permute-start(f32[16,2,8,256]{3,2,1,0:T(8,128)S(1)} %all_to_all.10), channel_id=1, source_target_pairs={{0,64},{32,96},{64,0},{96,32},{1,65},{33,97},{65,1},{97,33},{2,66}... | collective-permute-start | bytes 786440 | tf_op jit(solution)/shard_map/ppermute | solution.py:112
  26.4 15.2 %collective-permute-start.2 = (f32[16,2,8,256]{3,2,1,0:T(8,128)S(1)}, f32[16,2,8,256]{3,2,1,0:T(8,128)S(1)}, u32[]{:S(2)}, u32[]{:S(2)}) collective-permute-start(f32[16,2,8,256]{3,2,1,0:T(8,128)S(1)} %collective-permute-done), channel_id=1, source_target_pairs={{0,32},{32,64},{64,96},{96,0},{1,33},{33,65},{65,97},{97,1},{2,34}... | collective-permute-start | bytes 786440 | tf_op jit(solution)/shard_map/ppermute | solution.py:112
  27.5 14.3 %collective-permute-start.4 = (f32[16,2,8,256]{3,2,1,0:T(8,128)S(1)}, f32[16,2,8,256]{3,2,1,0:T(8,128)S(1)}, u32[]{:S(2)}, u32[]{:S(2)}) collective-permute-start(f32[16,2,8,256]{3,2,1,0:T(8,128)S(1)} %collective-permute-done), channel_id=1, source_target_pairs={{0,96},{32,0},{64,32},{96,64},{1,97},{33,1},{65,33},{97,65},{2,98}... | collective-permute-start | bytes 786440 | tf_op jit(solution)/shard_map/ppermute | solution.py:112
  29.2 16.9 %collective-permute-start.6 = (f32[16,2,8,256]{3,2,1,0:T(8,128)S(1)}, f32[16,2,8,256]{3,2,1,0:T(8,128)S(1)}, u32[]{:S(2)}, u32[]{:S(2)}) collective-permute-start(f32[16,2,8,256]{3,2,1,0:T(8,128)S(1)} %collective-permute-done), channel_id=1, source_target_pairs={{0,64},{32,96},{64,0},{96,32},{1,65},{33,97},{65,1},{97,33},{2,66}... | collective-permute-start | bytes 786440 | tf_op jit(solution)/shard_map/ppermute | solution.py:112
  46.1 7.8 %collective-permute-start.7 = (f32[8,16,2,8,256]{4,3,2,1,0:T(8,128)S(1)}, f32[8,16,2,8,256]{4,3,2,1,0:T(8,128)}, u32[]{:S(2)}, u32[]{:S(2)}) collective-permute-start(f32[8,16,2,8,256]{4,3,2,1,0:T(8,128)S(1)} %bitcast_dynamic-update-slice_fusion.x_same), channel_id=1, source_target_pairs={{0,1},{1,0},{2,3},{3,2},{4,5},{5,4},{6,7},{7,6},{8,9},{9,8},{10,11... | collective-permute-start | bytes 6291464 | tf_op jit(solution)/shard_map/ppermute | solution.py:96
  53.9 2.8 %copy-start = (f32[1,1,8,3,256,256]{5,4,3,2,1,0:T(8,128)S(1)}, f32[1,1,8,3,256,256]{5,4,3,2,1,0:T(8,128)}, u32[]{:S(2)}) copy-start(f32[1,1,8,3,256,256]{5,4,3,2,1,0:T(8,128)} %param.10) | copy-start | bytes 18874372
  56.7 2.8 %copy-start.1 = (f32[1,1,8,3,256,256]{5,4,3,2,1,0:T(8,128)S(1)}, f32[1,1,8,3,256,256]{5,4,3,2,1,0:T(8,128)}, u32[]{:S(2)}) copy-start(f32[1,1,8,3,256,256]{5,4,3,2,1,0:T(8,128)} %param.11) | copy-start | bytes 18874372
  73.2 3.3 %collective-permute-start.8 = (f32[16,2,8,256]{3,2,1,0:T(8,128)S(1)}, f32[16,2,8,256]{3,2,1,0:T(8,128)S(1)}, u32[]{:S(2)}, u32[]{:S(2)}) collective-permute-start(f32[16,2,8,256]{3,2,1,0:T(8,128)S(1)} %get-tuple-element.8), channel_id=1, source_target_pairs={{0,1},{1,0},{2,3},{3,2},{4,5},{5,4},{6,7},{7,6},{8,9},{9,8},{10,11... | collective-permute-start | bytes 786440 | tf_op jit(solution)/shard_map/ppermute | solution.py:96
  77.2 13.4 %all-to-all-start.1 = ((f32[16,2,8,256]{3,2,1,0:T(8,128)}), f32[16,2,8,256]{3,2,1,0:T(8,128)S(1)}, u32[]{:S(2)}, u32[]{:S(2)}) async-start(f32[16,2,8,256]{3,2,1,0:T(8,128)} %add.76), calls=%async_computation.1 | async-start | bytes 524288 | tf_op jit(solution)/shard_map/all_to_all | solution.py:122

commit v2 on v1

v2 whole, which is shorter than its diff:
```python
import functools

import jax
import jax.numpy as jnp
from jax import lax
from jax.experimental import pallas as pl
from jax.experimental.pallas import tpu as pltpu
from jax.sharding import Mesh, PartitionSpec as P

GROUPS, PAIRS, SLOTS, STATES, ROWS = 8, 2, 3, 256, 8
RUNS = STATES // (2 * ROWS)
F32, BF16 = jnp.float32, jnp.bfloat16
SUMS = (PAIRS, STATES, STATES)
AHEAD = 1
STEPS = (0, 1, 3, 2)
LIMIT = 48 * 2**20
LONG = 20 * 10**9
HALF = (RUNS, PAIRS, ROWS, STATES)


def split(value):
    high = value.astype(BF16)
    return high, (value - high.astype(F32)).astype(BF16)


def dot3(left, right, contract):
    dot = functools.partial(
        lax.dot_general, dimension_numbers=(contract, ((), ())), preferred_element_type=F32
    )
    return dot(left[0], right[0]) + dot(left[0], right[1]) + dot(left[1], right[0])


def interleave(even, odd):
    return jnp.stack([even, odd], axis=1).reshape(STATES, STATES)


def chunk_kernel(parts, sizes, codes, scales, *refs):
    panels, refs = refs[: 4 * parts], refs[4 * parts :]
    left, right, keep, give, total, x_high, x_low, lefts, rights, done = refs
    core, my_y, my_x = lax.axis_index("core"), lax.axis_index("y_hi"), lax.axis_index("x")
    sources = [
        y * 4 + lax.rem(my_x + 4 - step, 4) for y in (my_y, 1 - my_y) for step in STEPS
    ]

    def env(j):
        source = sources[j]
        return (
            pltpu.make_async_copy(left.at[source], lefts.at[j], done.at[j, 0]),
            pltpu.make_async_copy(right.at[source], rights.at[j], done.at[j, 1]),
        )

    def fetch(j):
        for copy in env(j):
            copy.start()

    row_ids = lax.broadcasted_iota(jnp.int32, (STATES, STATES), 0)
    col_ids = lax.broadcasted_iota(jnp.int32, (STATES, STATES), 1)

    def rows(j):
        for pair in range(PAIRS):
            (same, at), (other, _) = panels[4 * j + 2 * pair : 4 * j + 2 * pair + 2]
            same, other = same[at], other[at]
            even = jnp.where(core == 0, same, other)
            odd = jnp.where(core == 0, other, same)
            here = sources[j] * PAIRS + pair
            valid = (row_ids < sizes[0, here]) & (col_ids < sizes[1, here])
            whole = jnp.where(valid, interleave(even, odd), 0.0)
            x_high[j % 2, pair], x_low[j % 2, pair] = split(whole)

    def products(j):
        inner = []
        for slot in range(SLOTS):
            pair = codes[0, slot, 0, sources[j]] // 2
            x = x_high[j % 2, pair], x_low[j % 2, pair]
            product = dot3(split(lefts[j, slot]), x, ((1,), (0,)))
            inner.append(split(product * scales[0, slot, 0, sources[j]]))
        return inner

    def add(j, inner):
        for slot in range(SLOTS):
            total[codes[0, slot, 0, sources[j]] % 2] += dot3(inner[slot], split(rights[j, slot]), ((1,), (1,)))

    for j in range(AHEAD):
        fetch(j)
    total[...] = jnp.zeros(SUMS, F32)
    rows(0)
    inner = None
    for j in range(parts + 1):
        if j + AHEAD < parts:
            fetch(j + AHEAD)
        if j < parts:
            env(j)[0].wait()
        if j > 0:
            env(j - 1)[1].wait()
        coming = products(j) if j < parts else None
        if j + 1 < parts:
            rows(j + 1)
        if j > 0:
            add(j - 1, inner)
        inner = coming
    for pair in range(PAIRS):
        pairs = total[pair].reshape(RUNS, 2, ROWS, STATES)
        keep[:, pair] = jnp.where(core == 0, pairs[:, 0], pairs[:, 1])
        give[:, pair] = jnp.where(core == 0, pairs[:, 1], pairs[:, 0])


def chunk(lists, panels, left, right, estimate):
    parts = len(panels) // 4
    smem, vmem, hbm = (
        pl.BlockSpec(memory_space=space)
        for space in (pltpu.SMEM, pltpu.VMEM, pl.ANY)
    )
    arrays = []
    for array, _ in panels:
        if not any(array is known for known in arrays):
            arrays.append(array)
    at = [[array is known for known in arrays].index(True) for array, _ in panels]

    def kernel(*refs):
        here = [(refs[3 + k], index) for k, (_, index) in zip(at, panels)]
        chunk_kernel(parts, *refs[:3], *here, *refs[3 + len(arrays) :])

    return pl.pallas_call(
        kernel,
        in_specs=[smem] * 3 + [vmem] * len(arrays) + [hbm] * 2,
        out_specs=[vmem] * 2,
        out_shape=[jax.ShapeDtypeStruct(HALF, F32)] * 2,
        scratch_shapes=[
            pltpu.VMEM(SUMS, F32),
            pltpu.VMEM((2,) + SUMS, BF16),
            pltpu.VMEM((2,) + SUMS, BF16),
            pltpu.VMEM((parts, SLOTS, STATES, STATES), F32),
            pltpu.VMEM((parts, SLOTS, STATES, STATES), F32),
            pltpu.SemaphoreType.DMA((parts, 2)),
        ],
        cost_estimate=pl.CostEstimate(flops=estimate, bytes_accessed=2**20, transcendentals=0),
        compiler_params=pltpu.CompilerParams(vmem_limit_bytes=LIMIT),
    )(*lists, *arrays, left, right)


def swap_core(value):
    return lax.ppermute(value, "core", [(0, 1), (1, 0)])


def ahead(value, step):
    return lax.ppermute(value, "x", [(x, (x + step) % 4) for x in range(4)])


def across(value):
    return lax.ppermute(value, "y_hi", [(0, 1), (1, 0)])


def local(
    wavefunction, sector_sizes, env_left, env_right, mpo_weight, bond_index, in_pair, out_pair
):
    core = lax.axis_index("core")
    my_y, my_x = lax.axis_index("y_hi"), lax.axis_index("x")
    left, right = env_left[0, 0], env_right[0, 0]

    runs = lax.all_to_all(
        jnp.broadcast_to(wavefunction[None], (RUNS,) + wavefunction.shape), ("y_lo", "z"), 0, 0
    )
    first, second = runs[None, :, 0], runs[None, :, 1]
    live = out_pair >= 0
    picked = bond_index[..., None] == jnp.arange(mpo_weight.shape[0], dtype=jnp.int32)
    scales = jnp.where(live, jnp.sum(jnp.where(picked, mpo_weight, 0.0), axis=-1), 0.0)
    codes = in_pair * 2 + jnp.maximum(out_pair, 0)
    lists = (
        jnp.minimum(sector_sizes.T, STATES),
        *[lax.transpose(array, (0, 3, 1, 2)) for array in (codes, scales)],
    )
    (crossed, *beside), lists = lax.optimization_barrier(
        ([across(first), *[ahead(second, step) for step in STEPS[1:]]], lists)
    )
    column = jnp.concatenate([first, crossed])
    row = jnp.concatenate([second, *beside])
    far_row = across(row)
    columns = [column] + [ahead(column, step) for step in STEPS[1:]]

    mid = jnp.concatenate(columns[1:])
    both = [(column, swap_core(column), 0)] + [(mid, swap_core(mid), 2 * k) for k in range(3)]
    panels = []
    for side, here in enumerate((row, far_row)):
        other = swap_core(here)
        for k in range(4):
            panels += [(array, both[k][2] + side) for array in both[k][:2]] + [(here, k), (other, k)]
    keep, give = chunk(lists, panels, left, right, LONG)
    half = keep + swap_core(give)
    summed = lax.all_to_all(half, ("y_lo", "z"), 0, 0).sum(0)

    owner = (lax.axis_index("y_lo") * 8 + lax.axis_index("z")) * 2 + core
    group_sizes = lax.dynamic_slice_in_dim(sector_sizes, (my_y * 4 + my_x) * PAIRS, PAIRS, 0)
    row_ids = owner * ROWS + jnp.arange(ROWS, dtype=jnp.int32)
    col_ids = jnp.arange(STATES, dtype=jnp.int32)
    valid = (row_ids[None, :, None] < group_sizes[:, 0, None, None]) & (
        col_ids[None, None, :] < group_sizes[:, 1, None, None]
    )
    return jnp.where(valid, summed, 0.0)


def solution(mesh):
    fine = Mesh(mesh.devices.reshape(2, 4, 2, 8, 2), ("y_hi", "x", "y_lo", "z", "core"))
    blk, sec = ("y_hi", "x"), ("y_lo", "z", "core")
    return jax.shard_map(
        local,
        mesh=fine,
        in_specs=(
            P(blk, sec, None),
            P(),
            P(blk, sec, None, None, None, None),
            P(blk, sec, None, None, None, None),
            P(),
            P(blk, sec, None, None),
            P(blk, sec, None, None),
            P(blk, sec, None, None),
        ),
        out_specs=P(blk, sec, None),
        check_vma=False,
    )
```

time: 92.5 us -> 81.9 us (0.89)
  blocking collectives: 18.7 us -> 0 us
  starting transfers between devices: 21.3 us -> 36.8 us
  local copies, waits for them, and re-layouts: 6.96 us -> 2.28 us
  waiting for transfers between devices: 28.9 us -> 25.3 us
  other arithmetic: 1.58 us -> 4.52 us
  Pallas kernels: 13.7 us -> 11.8 us
    all_to_all x1 -> x0, blocking collectives: 18.7 us -> none  [local(): lax.all_to_all(jnp.broadcast_to(wavefunction[None], (RUNS,) + wavefunctio...]
    all_to_all x0 -> x1, starting transfers between devices: none -> 10.1 us  [local(): lax.all_to_all(jnp.broadcast_to(wavefunction[None], (RUNS,) + wavefunctio...]
    ppermute x7 -> x8, waiting for transfers between devices: 15.3 us -> 7.33 us  [the longest x6 6.41 us: ahead(): return lax.ppermute(value, 'x', [(x, (x + step) % 4) for x in range(4)])]
    all_to_all x0 -> x1, waiting for transfers between devices: none -> 5.85 us  [local(): lax.all_to_all(jnp.broadcast_to(wavefunction[None], (RUNS,) + wavefunctio...]
    unnamed x22 -> x5, local copies, waits for them, and re-layouts: 5.81 us -> 0.72 us
    ppermute x2 -> x5, starting transfers between devices: 6.03 us -> 8.35 us  [swap_core(): return lax.ppermute(value, 'core', [(0, 1), (1, 0)])]
    pallas_call x1, Pallas kernels: 13.7 us -> 11.8 us  [chunk(): pl.pallas_call(kernel, in_specs=[smem] * 3 + [vmem] * len(arrays) + [hbm]...]
    ppermute x7 -> x8, starting transfers between devices: 11.1 us -> 12.6 us  [the longest x6 7.27 us: ahead(): return lax.ppermute(value, 'x', [(x, (x + step) % 4) for x in range(4)])]
  transfers between devices with their start and end apart: 10 -> 15, of which waited for: 5 -> 10; matrix products, arithmetic and copies ran while one was open for 1% -> 5% of each run, Pallas kernels for 0% -> 0%
where the time goes in v2:
time: 81.9 us; the launch traced here: 80.7 us
  starting transfers between devices  36.8 us (45%)
  waiting for transfers between devices  25.3 us (31%)
  Pallas kernels  11.8 us (14%)
  other arithmetic  4.52 us (6%)
  local copies, waits for them, and re-layouts  2.28 us (3%)
    pallas_call x1, Pallas kernels, chunk(): pl.pallas_call(kernel, in_specs=[smem] * 3 + [vmem] * len(arrays) + [hbm]...  11.8 us
    all_to_all x1, starting transfers between devices, local(): lax.all_to_all(jnp.broadcast_to(wavefunction[None], (RUNS,) + wavefunctio...  10.1 us
    all_to_all x1, waiting for transfers between devices, local(): summed = lax.all_to_all(half, ('y_lo', 'z'), 0, 0).sum(0)  8.78 us
    ppermute x5, starting transfers between devices, swap_core(): return lax.ppermute(value, 'core', [(0, 1), (1, 0)])  8.35 us
    ppermute x6, starting transfers between devices, ahead(): return lax.ppermute(value, 'x', [(x, (x + step) % 4) for x in range(4)])  7.27 us
    ppermute x6, waiting for transfers between devices, ahead(): return lax.ppermute(value, 'x', [(x, (x + step) % 4) for x in range(4)])  6.41 us
    all_to_all x1, waiting for transfers between devices, local(): lax.all_to_all(jnp.broadcast_to(wavefunction[None], (RUNS,) + wavefunctio...  5.85 us
    all_to_all x1, starting transfers between devices, local(): summed = lax.all_to_all(half, ('y_lo', 'z'), 0, 0).sum(0)  5.69 us
  transfers between devices with their start and end apart: 15, of which 10 were waited for; matrix products, arithmetic and copies ran while one was open for 5% of the time, Pallas kernels for 0%

profile of v2, /device:TPU:1, one launch (start us, length us, event | category | flops | bytes accessed | tf_op | source)
XLA Modules:
  0.0 80.7 jit_solution(11720498136423314241)
XLA Ops:
  0.0 1.4 %broadcast_in_dim.26 = f32[16,2,8,256]{3,2,1,0:T(8,128)} broadcast(f32[2,8,256]{2,1,0:T(8,128)} %param.8), dimensions={1,2,3} | broadcast | bytes 278528 | tf_op jit(solution)/shard_map/broadcast_in_dim | solution.py:161
  1.4 10.1 %all-to-all-start = ((f32[16,2,8,256]{3,2,1,0:T(8,128)}), f32[16,2,8,256]{3,2,1,0:T(8,128)S(1)}, u32[]{:S(2)}, u32[]{:S(2)}) async-start(f32[16,2,8,256]{3,2,1,0:T(8,128)} %broadcast_in_dim.26), calls=%async_computation | async-start | bytes 524288 | tf_op jit(solution)/shard_map/all_to_all | solution.py:160
  11.6 0.7 copy.23
  12.3 0.8 %select_reduce_fusion = f32[8,3]{0,1:T(4,128)S(1)} fusion(f32[26]{0:T(128)} %param.12, s32[8,3]{0,1:T(4,128)S(1)} %bitcast.24), kind=kLoop, calls=%fused_computation.5 | loop fusion | flops 1848 | bytes 296 | tf_op jit(solution)/shard_map/reduce_sum | solution.py:166
  13.1 0.7 fusion.refs_2_
  13.8 0.7 add_bitcast_fusion.refs_1_
  14.5 5.8 %all-to-all-done = f32[16,2,8,256]{3,2,1,0:T(8,128)S(1)} async-done(((f32[16,2,8,256]{3,2,1,0:T(8,128)}), f32[16,2,8,256]{3,2,1,0:T(8,128)S(1)}, u32[]{:S(2)}, u32[]{:S(2)}) %all-to-all-start) | async-done | bytes 262176 | tf_op jit(solution)/shard_map/all_to_all | solution.py:160
  20.3 1.3 %collective-permute-start.1 = (f32[1,16,8,256]{3,2,1,0:T(8,128)S(1)}, f32[1,16,8,256]{3,2,1,0:T(8,128)S(1)}, u32[]{:S(2)}, u32[]{:S(2)}) collective-permute-start(f32[1,16,8,256]{3,2,1,0:T(8,128)S(1)} %get-tuple-element.23), channel_id=1, source_target_pairs={{0,32},{32,64},{64,96},{96,0},{1,33},{33,65},{65,97},{97,1},{2,34}... | collective-permute-start | bytes 393224 | tf_op jit(solution)/shard_map/ppermute | solution.py:146
  21.6 1.5 %collective-permute-start.2 = (f32[1,16,8,256]{3,2,1,0:T(8,128)S(1)}, f32[1,16,8,256]{3,2,1,0:T(8,128)S(1)}, u32[]{:S(2)}, u32[]{:S(2)}) collective-permute-start(f32[1,16,8,256]{3,2,1,0:T(8,128)S(1)} %get-tuple-element.23), channel_id=1, source_target_pairs={{0,96},{32,0},{64,32},{96,64},{1,97},{33,1},{65,33},{97,65},{2,98}... | collective-permute-start | bytes 393224 | tf_op jit(solution)/shard_map/ppermute | solution.py:146
  23.1 1.5 %collective-permute-start.3 = (f32[1,16,8,256]{3,2,1,0:T(8,128)S(1)}, f32[1,16,8,256]{3,2,1,0:T(8,128)S(1)}, u32[]{:S(2)}, u32[]{:S(2)}) collective-permute-start(f32[1,16,8,256]{3,2,1,0:T(8,128)S(1)} %get-tuple-element.23), channel_id=1, source_target_pairs={{0,64},{32,96},{64,0},{96,32},{1,65},{33,97},{65,1},{97,33},{2,66}... | collective-permute-start | bytes 393224 | tf_op jit(solution)/shard_map/ppermute | solution.py:146
  24.6 2.6 %collective-permute-start = (f32[1,16,8,256]{3,2,1,0:T(8,128)S(1)}, f32[1,16,8,256]{3,2,1,0:T(8,128)S(1)}, u32[]{:S(2)}, u32[]{:S(2)}) collective-permute-start(f32[1,16,8,256]{3,2,1,0:T(8,128)S(1)} %get-tuple-element.24), channel_id=1, source_target_pairs={{0,128},{128,0},{1,129},{129,1},{2,130},{130,2},{3,131},{131,3},{4... | collective-permute-start | bytes 393224 | tf_op jit(solution)/shard_map/ppermute | solution.py:150
  27.2 0.7 minimum_bitcast_fusion.refs_0_
  27.9 0.0 collective-permute-done.1
  27.9 0.0 collective-permute-done.2
  27.9 1.1 %collective-permute-done.3 = f32[1,16,8,256]{3,2,1,0:T(8,128)S(1)} collective-permute-done((f32[1,16,8,256]{3,2,1,0:T(8,128)S(1)}, f32[1,16,8,256]{3,2,1,0:T(8,128)S(1)}, u32[]{:S(2)}, u32[]{:S(2)}) %collective-permute-start.3) | collective-permute-done | bytes 131104 | tf_op jit(solution)/shard_map/ppermute | solution.py:146
  29.0 0.9 %collective-permute-done = f32[1,16,8,256]{3,2,1,0:T(8,128)S(1)} collective-permute-done((f32[1,16,8,256]{3,2,1,0:T(8,128)S(1)}, f32[1,16,8,256]{3,2,1,0:T(8,128)S(1)}, u32[]{:S(2)}, u32[]{:S(2)}) %collective-permute-start) | collective-permute-done | bytes 131104 | tf_op jit(solution)/shard_map/ppermute | solution.py:150
  30.0 0.4 collective-permute-start.6
  30.4 2.4 %collective-permute-start.7 = (f32[2,16,8,256]{3,2,1,0:T(8,128)S(1)}, f32[2,16,8,256]{3,2,1,0:T(8,128)S(1)}, u32[]{:S(2)}, u32[]{:S(2)}) collective-permute-start(f32[2,16,8,256]{3,2,1,0:T(8,128)S(1)} %pad_maximum_fusion.1.refs_3_), channel_id=1, source_target_pairs={{0,96},{32,0},{64,32},{96,64},{1,97},{33,1},{65,33},{97,65},{2,98}... | collective-permute-start | bytes 786440 | tf_op jit(solution)/shard_map/ppermute | solution.py:146
  32.7 0.2 collective-permute-start.8
  33.0 2.7 %collective-permute-start.10 = (f32[4,16,8,256]{3,2,1,0:T(8,128)S(1)}, f32[4,16,8,256]{3,2,1,0:T(8,128)S(1)}, u32[]{:S(2)}, u32[]{:S(2)}) collective-permute-start(f32[4,16,8,256]{3,2,1,0:T(8,128)S(1)} %pad_maximum_fusion.refs_5_), channel_id=1, source_target_pairs={{0,128},{128,0},{1,129},{129,1},{2,130},{130,2},{3,131},{131,3},{4... | collective-permute-start | bytes 1572872 | tf_op jit(solution)/shard_map/ppermute | solution.py:150
  35.7 0.8 collective-permute-done.6
  36.5 2.7 %collective-permute-done.7 = f32[2,16,8,256]{3,2,1,0:T(8,128)S(1)} collective-permute-done((f32[2,16,8,256]{3,2,1,0:T(8,128)S(1)}, f32[2,16,8,256]{3,2,1,0:T(8,128)S(1)}, u32[]{:S(2)}, u32[]{:S(2)}) %collective-permute-start.7) | collective-permute-done | bytes 262176 | tf_op jit(solution)/shard_map/ppermute | solution.py:146
  39.2 1.8 %collective-permute-done.8 = f32[2,16,8,256]{3,2,1,0:T(8,128)S(1)} collective-permute-done((f32[2,16,8,256]{3,2,1,0:T(8,128)S(1)}, f32[2,16,8,256]{3,2,1,0:T(8,128)S(1)}, u32[]{:S(2)}, u32[]{:S(2)}) %collective-permute-start.8) | collective-permute-done | bytes 262176 | tf_op jit(solution)/shard_map/ppermute | solution.py:146
  41.1 5.2 %collective-permute-start.9 = (f32[6,16,8,256]{3,2,1,0:T(8,128)S(1)}, f32[6,16,8,256]{3,2,1,0:T(8,128)S(1)}, u32[]{:S(2)}, u32[]{:S(2)}) collective-permute-start(f32[6,16,8,256]{3,2,1,0:T(8,128)S(1)} %constant_dynamic-update-slice_fusion.refs_7_), channel_id=1, source_target_pairs={{0,1},{1,0},{2,3},{3,2},{4,5},{5,4},{6,7},{7,6},{8,9},{9,8},{10,11... | collective-permute-start | bytes 2359304 | tf_op jit(solution)/shard_map/ppermute | solution.py:142
  46.2 0.1 collective-permute-start.5
  46.3 0.0 collective-permute-done.10.refs_11_
  46.4 2.6 %collective-permute-start.11 = (f32[4,16,8,256]{3,2,1,0:T(8,128)S(1)}, f32[4,16,8,256]{3,2,1,0:T(8,128)}, u32[]{:S(2)}, u32[]{:S(2)}) collective-permute-start(f32[4,16,8,256]{3,2,1,0:T(8,128)S(1)} %collective-permute-done.10.refs_11_), channel_id=1, source_target_pairs={{0,1},{1,0},{2,3},{3,2},{4,5},{5,4},{6,7},{7,6},{8,9},{9,8},{10,11... | collective-permute-start | bytes 1572872 | tf_op jit(solution)/shard_map/ppermute | solution.py:142
  48.9 0.0 collective-permute-start.4
  48.9 1.8 %collective-permute-done.4.refs_4_ = f32[2,16,8,256]{3,2,1,0:T(8,128)S(1)} collective-permute-done((f32[2,16,8,256]{3,2,1,0:T(8,128)S(1)}, f32[2,16,8,256]{3,2,1,0:T(8,128)S(1)}, u32[]{:S(2)}, u32[]{:S(2)}) %collective-permute-start.4) | collective-permute-done | bytes 262176 | tf_op jit(solution)/shard_map/ppermute | solution.py:142
  50.7 0.0 collective-permute-done.5.refs_6_
  50.7 0.0 collective-permute-done.9.refs_8_.refs_9_.refs_10_
  50.7 0.3 collective-permute-done.11.refs_12_
  51.0 0.0 copy-start
  51.0 11.8 %shard_map.82 = (f32[16,2,8,256]{3,2,1,0:T(8,128)S(1)}, f32[16,2,8,256]{3,2,1,0:T(8,128)}) custom-call(s32[2,16]{1,0:T(2,128)S(1)} %minimum_bitcast_fusion.refs_0_, s32[1,3,1,8]{3,2,1,0:T(1,128)S(1)} %add_bitcast_fusion.refs_1_, f32[1,3,1,8]{3,2,1,0:T(1,128)S(1)} %fusion.refs_2_, f32[2,16,8,256]{3,2,1,0:T(8,128)S(1)} %pad_maximum_fusion.1.refs_3_, ...), custom_call_target="tpu_custom_call" | custom-call | flops 20000000000 | bytes 1048576 | tf_op jit(solution)/shard_map/pallas_call | solution.py:123
  62.8 0.5 collective-permute-start.12
  63.3 0.0 copy-done
  63.3 0.1 constant_dynamic-slice_fusion
  63.4 1.3 %collective-permute-done.12 = f32[16,2,8,256]{3,2,1,0:T(8,128)S(1)} collective-permute-done((f32[16,2,8,256]{3,2,1,0:T(8,128)}, f32[16,2,8,256]{3,2,1,0:T(8,128)S(1)}, u32[]{:S(2)}, u32[]{:S(2)}) %collective-permute-start.12) | collective-permute-done | bytes 262176 | tf_op jit(solution)/shard_map/ppermute | solution.py:142
  64.7 0.7 add.35
  65.4 5.7 %all-to-all-start.1 = ((f32[16,2,8,256]{3,2,1,0:T(8,128)}), f32[16,2,8,256]{3,2,1,0:T(8,128)S(1)}, u32[]{:S(2)}, u32[]{:S(2)}) async-start(f32[16,2,8,256]{3,2,1,0:T(8,128)} %add.35), calls=%async_computation.1 | async-start | bytes 524288 | tf_op jit(solution)/shard_map/all_to_all | solution.py:189
  71.1 0.1 iota_compare_fusion.1
  71.2 0.1 broadcast_compare_fusion
  71.3 8.8 %all-to-all-done.1 = f32[16,2,8,256]{3,2,1,0:T(8,128)S(1)} async-done(((f32[16,2,8,256]{3,2,1,0:T(8,128)}), f32[16,2,8,256]{3,2,1,0:T(8,128)S(1)}, u32[]{:S(2)}, u32[]{:S(2)}) %all-to-all-start.1) | async-done | bytes 262176 | tf_op jit(solution)/shard_map/all_to_all | solution.py:189
  80.1 0.7 and_select_fusion
  (9 shorter events, 0.2 us)
Async XLA Ops:
  1.4 18.9 %all-to-all-start = ((f32[16,2,8,256]{3,2,1,0:T(8,128)}), f32[16,2,8,256]{3,2,1,0:T(8,128)S(1)}, u32[]{:S(2)}, u32[]{:S(2)}) async-start(f32[16,2,8,256]{3,2,1,0:T(8,128)} %broadcast_in_dim.26), calls=%async_computation | async-start | bytes 524288 | tf_op jit(solution)/shard_map/all_to_all | solution.py:160
  20.3 7.6 %collective-permute-start.1 = (f32[1,16,8,256]{3,2,1,0:T(8,128)S(1)}, f32[1,16,8,256]{3,2,1,0:T(8,128)S(1)}, u32[]{:S(2)}, u32[]{:S(2)}) collective-permute-start(f32[1,16,8,256]{3,2,1,0:T(8,128)S(1)} %get-tuple-element.23), channel_id=1, source_target_pairs={{0,32},{32,64},{64,96},{96,0},{1,33},{33,65},{65,97},{97,1},{2,34}... | collective-permute-start | bytes 393224 | tf_op jit(solution)/shard_map/ppermute | solution.py:146
  21.6 6.3 %collective-permute-start.2 = (f32[1,16,8,256]{3,2,1,0:T(8,128)S(1)}, f32[1,16,8,256]{3,2,1,0:T(8,128)S(1)}, u32[]{:S(2)}, u32[]{:S(2)}) collective-permute-start(f32[1,16,8,256]{3,2,1,0:T(8,128)S(1)} %get-tuple-element.23), channel_id=1, source_target_pairs={{0,96},{32,0},{64,32},{96,64},{1,97},{33,1},{65,33},{97,65},{2,98}... | collective-permute-start | bytes 393224 | tf_op jit(solution)/shard_map/ppermute | solution.py:146
  23.1 5.9 %collective-permute-start.3 = (f32[1,16,8,256]{3,2,1,0:T(8,128)S(1)}, f32[1,16,8,256]{3,2,1,0:T(8,128)S(1)}, u32[]{:S(2)}, u32[]{:S(2)}) collective-permute-start(f32[1,16,8,256]{3,2,1,0:T(8,128)S(1)} %get-tuple-element.23), channel_id=1, source_target_pairs={{0,64},{32,96},{64,0},{96,32},{1,65},{33,97},{65,1},{97,33},{2,66}... | collective-permute-start | bytes 393224 | tf_op jit(solution)/shard_map/ppermute | solution.py:146
  24.6 5.3 %collective-permute-start = (f32[1,16,8,256]{3,2,1,0:T(8,128)S(1)}, f32[1,16,8,256]{3,2,1,0:T(8,128)S(1)}, u32[]{:S(2)}, u32[]{:S(2)}) collective-permute-start(f32[1,16,8,256]{3,2,1,0:T(8,128)S(1)} %get-tuple-element.24), channel_id=1, source_target_pairs={{0,128},{128,0},{1,129},{129,1},{2,130},{130,2},{3,131},{131,3},{4... | collective-permute-start | bytes 393224 | tf_op jit(solution)/shard_map/ppermute | solution.py:150
  30.0 6.5 %collective-permute-start.6 = (f32[2,16,8,256]{3,2,1,0:T(8,128)S(1)}, f32[2,16,8,256]{3,2,1,0:T(8,128)S(1)}, u32[]{:S(2)}, u32[]{:S(2)}) collective-permute-start(f32[2,16,8,256]{3,2,1,0:T(8,128)S(1)} %pad_maximum_fusion.1.refs_3_), channel_id=1, source_target_pairs={{0,32},{32,64},{64,96},{96,0},{1,33},{33,65},{65,97},{97,1},{2,34}... | collective-permute-start | bytes 786440 | tf_op jit(solution)/shard_map/ppermute | solution.py:146
  30.4 8.8 %collective-permute-start.7 = (f32[2,16,8,256]{3,2,1,0:T(8,128)S(1)}, f32[2,16,8,256]{3,2,1,0:T(8,128)S(1)}, u32[]{:S(2)}, u32[]{:S(2)}) collective-permute-start(f32[2,16,8,256]{3,2,1,0:T(8,128)S(1)} %pad_maximum_fusion.1.refs_3_), channel_id=1, source_target_pairs={{0,96},{32,0},{64,32},{96,64},{1,97},{33,1},{65,33},{97,65},{2,98}... | collective-permute-start | bytes 786440 | tf_op jit(solution)/shard_map/ppermute | solution.py:146
  32.7 8.3 %collective-permute-start.8 = (f32[2,16,8,256]{3,2,1,0:T(8,128)S(1)}, f32[2,16,8,256]{3,2,1,0:T(8,128)S(1)}, u32[]{:S(2)}, u32[]{:S(2)}) collective-permute-start(f32[2,16,8,256]{3,2,1,0:T(8,128)S(1)} %pad_maximum_fusion.1.refs_3_), channel_id=1, source_target_pairs={{0,64},{32,96},{64,0},{96,32},{1,65},{33,97},{65,1},{97,33},{2,66}... | collective-permute-start | bytes 786440 | tf_op jit(solution)/shard_map/ppermute | solution.py:146
  33.0 13.4 %collective-permute-start.10 = (f32[4,16,8,256]{3,2,1,0:T(8,128)S(1)}, f32[4,16,8,256]{3,2,1,0:T(8,128)S(1)}, u32[]{:S(2)}, u32[]{:S(2)}) collective-permute-start(f32[4,16,8,256]{3,2,1,0:T(8,128)S(1)} %pad_maximum_fusion.refs_5_), channel_id=1, source_target_pairs={{0,128},{128,0},{1,129},{129,1},{2,130},{130,2},{3,131},{131,3},{4... | collective-permute-start | bytes 1572872 | tf_op jit(solution)/shard_map/ppermute | solution.py:150
  41.1 9.6 %collective-permute-start.9 = (f32[6,16,8,256]{3,2,1,0:T(8,128)S(1)}, f32[6,16,8,256]{3,2,1,0:T(8,128)S(1)}, u32[]{:S(2)}, u32[]{:S(2)}) collective-permute-start(f32[6,16,8,256]{3,2,1,0:T(8,128)S(1)} %constant_dynamic-update-slice_fusion.refs_7_), channel_id=1, source_target_pairs={{0,1},{1,0},{2,3},{3,2},{4,5},{5,4},{6,7},{7,6},{8,9},{9,8},{10,11... | collective-permute-start | bytes 2359304 | tf_op jit(solution)/shard_map/ppermute | solution.py:142
  46.2 4.5 %collective-permute-start.5 = (f32[4,16,8,256]{3,2,1,0:T(8,128)S(1)}, f32[4,16,8,256]{3,2,1,0:T(8,128)}, u32[]{:S(2)}, u32[]{:S(2)}) collective-permute-start(f32[4,16,8,256]{3,2,1,0:T(8,128)S(1)} %pad_maximum_fusion.refs_5_), channel_id=1, source_target_pairs={{0,1},{1,0},{2,3},{3,2},{4,5},{5,4},{6,7},{7,6},{8,9},{9,8},{10,11... | collective-permute-start | bytes 1572872 | tf_op jit(solution)/shard_map/ppermute | solution.py:142
  46.4 4.6 %collective-permute-start.11 = (f32[4,16,8,256]{3,2,1,0:T(8,128)S(1)}, f32[4,16,8,256]{3,2,1,0:T(8,128)}, u32[]{:S(2)}, u32[]{:S(2)}) collective-permute-start(f32[4,16,8,256]{3,2,1,0:T(8,128)S(1)} %collective-permute-done.10.refs_11_), channel_id=1, source_target_pairs={{0,1},{1,0},{2,3},{3,2},{4,5},{5,4},{6,7},{7,6},{8,9},{9,8},{10,11... | collective-permute-start | bytes 1572872 | tf_op jit(solution)/shard_map/ppermute | solution.py:142
  48.9 1.8 %collective-permute-start.4 = (f32[2,16,8,256]{3,2,1,0:T(8,128)S(1)}, f32[2,16,8,256]{3,2,1,0:T(8,128)S(1)}, u32[]{:S(2)}, u32[]{:S(2)}) collective-permute-start(f32[2,16,8,256]{3,2,1,0:T(8,128)S(1)} %pad_maximum_fusion.1.refs_3_), channel_id=1, source_target_pairs={{0,1},{1,0},{2,3},{3,2},{4,5},{5,4},{6,7},{7,6},{8,9},{9,8},{10,11... | collective-permute-start | bytes 786440 | tf_op jit(solution)/shard_map/ppermute | solution.py:142
  51.0 12.3 %copy-start = (s32[16,2]{0,1:T(2,128)S(1)}, s32[16,2]{0,1:T(2,128)}, u32[]{:S(2)}) copy-start(s32[16,2]{0,1:T(2,128)} %param.9) | copy-start | bytes 388
  62.8 1.9 %collective-permute-start.12 = (f32[16,2,8,256]{3,2,1,0:T(8,128)}, f32[16,2,8,256]{3,2,1,0:T(8,128)S(1)}, u32[]{:S(2)}, u32[]{:S(2)}) collective-permute-start(f32[16,2,8,256]{3,2,1,0:T(8,128)} %get-tuple-element.22), channel_id=1, source_target_pairs={{0,1},{1,0},{2,3},{3,2},{4,5},{5,4},{6,7},{7,6},{8,9},{9,8},{10,11... | collective-permute-start | bytes 786440 | tf_op jit(solution)/shard_map/ppermute | solution.py:142
  65.4 14.6 %all-to-all-start.1 = ((f32[16,2,8,256]{3,2,1,0:T(8,128)}), f32[16,2,8,256]{3,2,1,0:T(8,128)S(1)}, u32[]{:S(2)}, u32[]{:S(2)}) async-start(f32[16,2,8,256]{3,2,1,0:T(8,128)} %add.35), calls=%async_computation.1 | async-start | bytes 524288 | tf_op jit(solution)/shard_map/all_to_all | solution.py:189

commit v3 on v2

v3 whole, which is shorter than its diff:
```python
import functools

import jax
import jax.numpy as jnp
from jax import lax
from jax.experimental import pallas as pl
from jax.experimental.pallas import tpu as pltpu
from jax.sharding import Mesh, PartitionSpec as P

GROUPS, PAIRS, SLOTS, STATES, ROWS = 8, 2, 3, 256, 8
RUNS = STATES // (2 * ROWS)
F32, BF16 = jnp.float32, jnp.bfloat16
SUMS = (PAIRS, STATES, STATES)
AHEAD = 2
STEPS = (0, 1, 3, 2)
LIMIT = 48 * 2**20
LONG = 20 * 10**9
HALF = (RUNS, PAIRS, ROWS, STATES)


def split(value):
    high = value.astype(BF16)
    return high, (value - high.astype(F32)).astype(BF16)


def dot3(left, right, contract):
    dot = functools.partial(
        lax.dot_general, dimension_numbers=(contract, ((), ())), preferred_element_type=F32
    )
    return dot(left[0], right[0]) + dot(left[0], right[1]) + dot(left[1], right[0])


def interleave(even, odd):
    return jnp.stack([even, odd], axis=1).reshape(STATES, STATES)


def chunk_kernel(parts, last, sizes, codes, scales, *refs):
    panels, refs = refs[: 4 * len(parts)], refs[4 * len(parts) :]
    left, right, *refs = refs
    if last:
        before, keep, give, total, *refs = refs
    else:
        total, *refs = refs
    x_high, x_low, lefts, rights, done = refs
    core, my_y, my_x = lax.axis_index("core"), lax.axis_index("y_hi"), lax.axis_index("x")
    sources = [
        (my_y, 1 - my_y)[side] * 4 + lax.rem(my_x + 4 - STEPS[k], 4) for side, k in parts
    ]

    def env(j):
        source = sources[j]
        return (
            pltpu.make_async_copy(left.at[source], lefts.at[j], done.at[j, 0]),
            pltpu.make_async_copy(right.at[source], rights.at[j], done.at[j, 1]),
        )

    def fetch(j):
        for copy in env(j):
            copy.start()

    row_ids = lax.broadcasted_iota(jnp.int32, (STATES, STATES), 0)
    col_ids = lax.broadcasted_iota(jnp.int32, (STATES, STATES), 1)

    def rows(j):
        for pair in range(PAIRS):
            same, other = [
                ref[at, :, pair] if whole else ref[at]
                for ref, at, whole in panels[4 * j + 2 * pair : 4 * j + 2 * pair + 2]
            ]
            even = jnp.where(core == 0, same, other)
            odd = jnp.where(core == 0, other, same)
            here = sources[j] * PAIRS + pair
            valid = (row_ids < sizes[0, here]) & (col_ids < sizes[1, here])
            x_high[j, pair], x_low[j, pair] = split(jnp.where(valid, interleave(even, odd), 0.0))

    for j in range(AHEAD):
        fetch(j)
    total[...] = before[...] if last else jnp.zeros(SUMS, F32)
    for j in range(len(parts)):
        rows(j)
    for j, source in enumerate(sources):
        if j + AHEAD < len(parts):
            fetch(j + AHEAD)
        for copy in env(j):
            copy.wait()
        inner = []
        for slot in range(SLOTS):
            pair = codes[0, slot, 0, source] // 2
            x = x_high[j, pair], x_low[j, pair]
            product = dot3(split(lefts[j, slot]), x, ((1,), (0,)))
            inner.append(split(product * scales[0, slot, 0, source]))
        for slot in range(SLOTS):
            target = codes[0, slot, 0, source] % 2
            total[target] += dot3(inner[slot], split(rights[j, slot]), ((1,), (1,)))
    if last:
        for pair in range(PAIRS):
            pairs = total[pair].reshape(RUNS, 2, ROWS, STATES)
            keep[:, pair] = jnp.where(core == 0, pairs[:, 0], pairs[:, 1])
            give[:, pair] = jnp.where(core == 0, pairs[:, 1], pairs[:, 0])


def chunk(parts, lists, panels, left, right, before):
    last = before is not None
    count = len(parts)
    smem, vmem, hbm = (
        pl.BlockSpec(memory_space=space) for space in (pltpu.SMEM, pltpu.VMEM, pl.ANY)
    )
    arrays = []
    for array, *_ in panels:
        if not any(array is known for known in arrays):
            arrays.append(array)
    at = [[array is known for known in arrays].index(True) for array, *_ in panels]

    def kernel(*refs):
        here = [(refs[3 + k], *panel[1:]) for k, panel in zip(at, panels)]
        chunk_kernel(parts, last, *refs[:3], *here, *refs[3 + len(arrays) :])

    result = pl.pallas_call(
        kernel,
        in_specs=[smem] * 3 + [vmem] * len(arrays) + [hbm] * 2 + [vmem] * last,
        out_specs=[vmem] * (2 if last else 1),
        out_shape=[jax.ShapeDtypeStruct(HALF, F32)] * 2
        if last
        else [jax.ShapeDtypeStruct(SUMS, F32)],
        scratch_shapes=[pltpu.VMEM(SUMS, F32)] * last
        + [
            pltpu.VMEM((count,) + SUMS, BF16),
            pltpu.VMEM((count,) + SUMS, BF16),
            pltpu.VMEM((count, SLOTS, STATES, STATES), F32),
            pltpu.VMEM((count, SLOTS, STATES, STATES), F32),
            pltpu.SemaphoreType.DMA((count, 2)),
        ],
        cost_estimate=pl.CostEstimate(flops=LONG if last else 10**9, bytes_accessed=2**20, transcendentals=0),
        compiler_params=pltpu.CompilerParams(vmem_limit_bytes=LIMIT),
    )(*lists, *arrays, left, right, *([before] if last else []))
    return result if last else result[0]


def swap_core(value):
    return lax.ppermute(value, "core", [(0, 1), (1, 0)])


def ahead(value, step):
    return lax.ppermute(value, "x", [(x, (x + step) % 4) for x in range(4)])


def across(value):
    return lax.ppermute(value, "y_hi", [(0, 1), (1, 0)])


def local(
    wavefunction, sector_sizes, env_left, env_right, mpo_weight, bond_index, in_pair, out_pair
):
    core = lax.axis_index("core")
    my_y, my_x = lax.axis_index("y_hi"), lax.axis_index("x")
    left, right = env_left[0, 0], env_right[0, 0]

    runs = lax.all_to_all(
        jnp.broadcast_to(wavefunction[None], (RUNS,) + wavefunction.shape), ("y_lo", "z"), 0, 0
    )
    runs = runs[None]
    live = out_pair >= 0
    picked = bond_index[..., None] == jnp.arange(mpo_weight.shape[0], dtype=jnp.int32)
    scales = jnp.where(live, jnp.sum(jnp.where(picked, mpo_weight, 0.0), axis=-1), 0.0)
    codes = in_pair * 2 + jnp.maximum(out_pair, 0)
    lists = (
        jnp.minimum(sector_sizes.T, STATES),
        *[lax.transpose(array, (0, 3, 1, 2)) for array in (codes, scales)],
    )
    (crossed, *beside), lists = lax.optimization_barrier(
        ([across(runs), *[ahead(runs, step) for step in STEPS[1:]]], lists)
    )
    near = jnp.concatenate([runs, *beside])
    far_first = [ahead(crossed[:, :, 0], step) for step in STEPS[1:]]
    far_second = across(near[1:, :, 1])

    near_other, crossed_other = swap_core(near), swap_core(crossed)
    parts = [(0, 0), (1, 0), (0, 1), (0, 2), (0, 3)]
    panels = []
    for side, k in parts:
        both = (near, near_other) if side == 0 else (crossed, crossed_other)
        panels += [(array, k, True) for array in both] * 2
    sums = chunk(parts, lists, panels, left, right, None)

    far_first, far_second, sums = lax.optimization_barrier((far_first, far_second, sums))
    far_first = jnp.concatenate(far_first)
    far = (far_first, swap_core(far_first), far_second, swap_core(far_second))
    parts = [(1, 1), (1, 2), (1, 3)]
    panels = [(array, k - 1, False) for _, k in parts for array in far]
    keep, give = chunk(parts, lists, panels, left, right, sums)
    half = keep + swap_core(give)
    summed = lax.all_to_all(half, ("y_lo", "z"), 0, 0).sum(0)

    owner = (lax.axis_index("y_lo") * 8 + lax.axis_index("z")) * 2 + core
    group_sizes = lax.dynamic_slice_in_dim(sector_sizes, (my_y * 4 + my_x) * PAIRS, PAIRS, 0)
    row_ids = owner * ROWS + jnp.arange(ROWS, dtype=jnp.int32)
    col_ids = jnp.arange(STATES, dtype=jnp.int32)
    valid = (row_ids[None, :, None] < group_sizes[:, 0, None, None]) & (
        col_ids[None, None, :] < group_sizes[:, 1, None, None]
    )
    return jnp.where(valid, summed, 0.0)


def solution(mesh):
    fine = Mesh(mesh.devices.reshape(2, 4, 2, 8, 2), ("y_hi", "x", "y_lo", "z", "core"))
    blk, sec = ("y_hi", "x"), ("y_lo", "z", "core")
    return jax.shard_map(
        local,
        mesh=fine,
        in_specs=(
            P(blk, sec, None),
            P(),
            P(blk, sec, None, None, None, None),
            P(blk, sec, None, None, None, None),
            P(),
            P(blk, sec, None, None),
            P(blk, sec, None, None),
            P(blk, sec, None, None),
        ),
        out_specs=P(blk, sec, None),
        check_vma=False,
    )
```

time: 81.9 us -> 77.9 us (0.951)
  starting transfers between devices: 36.8 us -> 31.3 us
  waiting for transfers between devices: 25.3 us -> 27.1 us
    ppermute x5, starting transfers between devices: 8.35 us -> 6.1 us  [swap_core(): return lax.ppermute(value, 'core', [(0, 1), (1, 0)])]
    ppermute x2, starting transfers between devices: 5.33 us -> 3.14 us  [across(): return lax.ppermute(value, 'y_hi', [(0, 1), (1, 0)])]
    all_to_all x1, starting transfers between devices: 5.69 us -> 4.77 us  [local(): summed = lax.all_to_all(half, ('y_lo', 'z'), 0, 0).sum(0)]
    ppermute x2, waiting for transfers between devices: 0.92 us -> 1.75 us  [across(): return lax.ppermute(value, 'y_hi', [(0, 1), (1, 0)])]
    pallas_call x1 -> x2, Pallas kernels: 11.8 us -> 11 us  [chunk(): pl.pallas_call(kernel, in_specs=[smem] * 3 + [vmem] * len(arrays) + [hbm]...]
  transfers between devices with their start and end apart: 15 -> 15, of which waited for: 10 -> 8; matrix products, arithmetic and copies ran while one was open for 5% -> 5% of each run, Pallas kernels for 0% -> 8%
where the time goes in v3:
time: 77.9 us; the launch traced here: 76.7 us
  starting transfers between devices  31.3 us (40%)
  waiting for transfers between devices  27.1 us (35%)
  Pallas kernels  11 us (14%)
  other arithmetic  4.57 us (6%)
  local copies, waits for them, and re-layouts  2.59 us (3%)
    pallas_call x2, Pallas kernels, chunk(): pl.pallas_call(kernel, in_specs=[smem] * 3 + [vmem] * len(arrays) + [hbm]...  11 us
    all_to_all x1, starting transfers between devices, local(): lax.all_to_all(jnp.broadcast_to(wavefunction[None], (RUNS,) + wavefunctio...  10.1 us
    all_to_all x1, waiting for transfers between devices, local(): summed = lax.all_to_all(half, ('y_lo', 'z'), 0, 0).sum(0)  8.78 us
    ppermute x6, starting transfers between devices, ahead(): return lax.ppermute(value, 'x', [(x, (x + step) % 4) for x in range(4)])  7.17 us
    ppermute x6, waiting for transfers between devices, ahead(): return lax.ppermute(value, 'x', [(x, (x + step) % 4) for x in range(4)])  7.11 us
    all_to_all x1, waiting for transfers between devices, local(): lax.all_to_all(jnp.broadcast_to(wavefunction[None], (RUNS,) + wavefunctio...  6.55 us
    ppermute x5, starting transfers between devices, swap_core(): return lax.ppermute(value, 'core', [(0, 1), (1, 0)])  6.1 us
    all_to_all x1, starting transfers between devices, local(): summed = lax.all_to_all(half, ('y_lo', 'z'), 0, 0).sum(0)  4.77 us
  transfers between devices with their start and end apart: 15, of which 8 were waited for; matrix products, arithmetic and copies ran while one was open for 5% of the time, Pallas kernels for 8%

profile of v3, /device:TPU:1, one launch (start us, length us, event | category | flops | bytes accessed | tf_op | source)
XLA Modules:
  0.0 76.7 jit_solution(13665813414878440439)
XLA Ops:
  0.0 1.4 %broadcast_in_dim.29 = f32[16,2,8,256]{3,2,1,0:T(8,128)} broadcast(f32[2,8,256]{2,1,0:T(8,128)} %param.8), dimensions={1,2,3} | broadcast | bytes 278528 | tf_op jit(solution)/shard_map/broadcast_in_dim | solution.py:159
  1.4 10.1 %all-to-all-start = ((f32[16,2,8,256]{3,2,1,0:T(8,128)}), f32[16,2,8,256]{3,2,1,0:T(8,128)S(1)}, u32[]{:S(2)}, u32[]{:S(2)}) async-start(f32[16,2,8,256]{3,2,1,0:T(8,128)} %broadcast_in_dim.29), calls=%async_computation | async-start | bytes 524288 | tf_op jit(solution)/shard_map/all_to_all | solution.py:158
  11.6 0.7 copy.33
  12.3 0.8 %select_reduce_fusion = f32[8,3]{0,1:T(4,128)S(1)} fusion(f32[26]{0:T(128)} %param.12, s32[8,3]{0,1:T(4,128)S(1)} %bitcast.32), kind=kLoop, calls=%fused_computation.7 | loop fusion | flops 1848 | bytes 296 | tf_op jit(solution)/shard_map/reduce_sum | solution.py:164
  13.1 0.7 fusion.1.refs_2_
  13.8 6.5 %all-to-all-done = f32[16,2,8,256]{3,2,1,0:T(8,128)S(1)} async-done(((f32[16,2,8,256]{3,2,1,0:T(8,128)}), f32[16,2,8,256]{3,2,1,0:T(8,128)S(1)}, u32[]{:S(2)}, u32[]{:S(2)}) %all-to-all-start) | async-done | bytes 262176 | tf_op jit(solution)/shard_map/all_to_all | solution.py:158
  20.3 2.7 %collective-permute-start = (f32[1,16,2,8,256]{4,3,1,0,2:T(8,128)S(1)}, f32[1,16,2,8,256]{4,3,1,0,2:T(8,128)S(1)}, u32[]{:S(2)}, u32[]{:S(2)}) collective-permute-start(f32[1,16,2,8,256]{4,3,1,0,2:T(8,128)S(1)} %bitcast.27), channel_id=1, source_target_pairs={{0,128},{128,0},{1,129},{129,1},{2,130},{130,2},{3,131},{131,3},{4... | collective-permute-start | bytes 786440 | tf_op jit(solution)/shard_map/ppermute | solution.py:148
  23.0 1.2 %collective-permute-start.1 = (f32[1,16,2,8,256]{4,3,1,0,2:T(8,128)S(1)}, f32[1,16,2,8,256]{4,3,1,0,2:T(8,128)S(1)}, u32[]{:S(2)}, u32[]{:S(2)}) collective-permute-start(f32[1,16,2,8,256]{4,3,1,0,2:T(8,128)S(1)} %bitcast.28), channel_id=1, source_target_pairs={{0,32},{32,64},{64,96},{96,0},{1,33},{33,65},{65,97},{97,1},{2,34}... | collective-permute-start | bytes 786440 | tf_op jit(solution)/shard_map/ppermute | solution.py:144
  24.3 1.5 %collective-permute-start.2 = (f32[1,16,2,8,256]{4,3,1,0,2:T(8,128)S(1)}, f32[1,16,2,8,256]{4,3,1,0,2:T(8,128)S(1)}, u32[]{:S(2)}, u32[]{:S(2)}) collective-permute-start(f32[1,16,2,8,256]{4,3,1,0,2:T(8,128)S(1)} %bitcast.29), channel_id=1, source_target_pairs={{0,96},{32,0},{64,32},{96,64},{1,97},{33,1},{65,33},{97,65},{2,98}... | collective-permute-start | bytes 786440 | tf_op jit(solution)/shard_map/ppermute | solution.py:144
  25.7 1.5 %collective-permute-start.3 = (f32[1,16,2,8,256]{4,3,1,0,2:T(8,128)S(1)}, f32[1,16,2,8,256]{4,3,1,0,2:T(8,128)S(1)}, u32[]{:S(2)}, u32[]{:S(2)}) collective-permute-start(f32[1,16,2,8,256]{4,3,1,0,2:T(8,128)S(1)} %bitcast.30), channel_id=1, source_target_pairs={{0,64},{32,96},{64,0},{96,32},{1,65},{33,97},{65,1},{97,33},{2,66}... | collective-permute-start | bytes 786440 | tf_op jit(solution)/shard_map/ppermute | solution.py:144
  27.3 0.7 minimum_bitcast_fusion.refs_0_
  27.9 0.7 add_bitcast_fusion.refs_1_
  28.6 0.0 collective-permute-done
  28.6 1.1 %collective-permute-done.1 = f32[1,16,2,8,256]{4,3,1,0,2:T(8,128)S(1)} collective-permute-done((f32[1,16,2,8,256]{4,3,1,0,2:T(8,128)S(1)}, f32[1,16,2,8,256]{4,3,1,0,2:T(8,128)S(1)}, u32[]{:S(2)}, u32[]{:S(2)}) %collective-permute-start.1) | collective-permute-done | bytes 262176 | tf_op jit(solution)/shard_map/ppermute | solution.py:144
  29.8 0.0 collective-permute-done.2
  29.8 6.0 %collective-permute-done.3 = f32[1,16,2,8,256]{4,3,1,0,2:T(8,128)S(1)} collective-permute-done((f32[1,16,2,8,256]{4,3,1,0,2:T(8,128)S(1)}, f32[1,16,2,8,256]{4,3,1,0,2:T(8,128)S(1)}, u32[]{:S(2)}, u32[]{:S(2)}) %collective-permute-start.3) | collective-permute-done | bytes 262176 | tf_op jit(solution)/shard_map/ppermute | solution.py:144
  35.7 0.1 pad_maximum_fusion
  35.8 3.9 %collective-permute-start.8 = (f32[4,16,2,8,256]{4,3,1,0,2:T(8,128)S(1)}, f32[4,16,2,8,256]{4,3,1,0,2:T(8,128)S(1)}, u32[]{:S(2)}, u32[]{:S(2)}) collective-permute-start(f32[4,16,2,8,256]{4,3,1,0,2:T(8,128)S(1)} %pad_maximum_fusion), channel_id=1, source_target_pairs={{0,1},{1,0},{2,3},{3,2},{4,5},{5,4},{6,7},{7,6},{8,9},{9,8},{10,11... | collective-permute-start | bytes 3145736 | tf_op jit(solution)/shard_map/ppermute | solution.py:140
  39.7 0.1 collective-permute-start.9
  39.9 0.4 collective-permute-start.7
  40.3 0.9 %collective-permute-start.4 = (f32[1,16,8,256]{3,2,1,0:T(8,128)S(1)}, f32[1,16,8,256]{3,2,1,0:T(8,128)S(1)}, u32[]{:S(2)}, u32[]{:S(2)}) collective-permute-start(f32[1,16,8,256]{3,2,1,0:T(8,128)S(1)} %slice_bitcast_fusion), channel_id=1, source_target_pairs={{0,32},{32,64},{64,96},{96,0},{1,33},{33,65},{65,97},{97,1},{2,34}... | collective-permute-start | bytes 393224 | tf_op jit(solution)/shard_map/ppermute | solution.py:144
  41.3 1.8 %collective-permute-start.5 = (f32[1,16,8,256]{3,2,1,0:T(8,128)S(1)}, f32[1,16,8,256]{3,2,1,0:T(8,128)S(1)}, u32[]{:S(2)}, u32[]{:S(2)}) collective-permute-start(f32[1,16,8,256]{3,2,1,0:T(8,128)S(1)} %slice_bitcast_fusion), channel_id=1, source_target_pairs={{0,96},{32,0},{64,32},{96,64},{1,97},{33,1},{65,33},{97,65},{2,98}... | collective-permute-start | bytes 393224 | tf_op jit(solution)/shard_map/ppermute | solution.py:144
  43.1 0.0 collective-permute-done.9
  43.1 0.2 collective-permute-start.6
  43.3 0.1 copy.24.refs_3_
  43.5 0.0 collective-permute-done.8
  43.5 0.1 copy.25.refs_4_
  43.6 6.3 %shard_map.82.refs_9_ = f32[2,256,256]{2,1,0:T(8,128)S(1)} custom-call(s32[2,16]{1,0:T(2,128)S(1)} %minimum_bitcast_fusion.refs_0_, s32[1,3,1,8]{3,2,1,0:T(1,128)S(1)} %add_bitcast_fusion.refs_1_, f32[1,3,1,8]{3,2,1,0:T(1,128)S(1)} %fusion.1.refs_2_, f32[4,16,2,8,256]{4,3,2,1,0:T(8,128)S(1)} %copy.24.refs_3_, f32[4,16,2,8,256]{4,3,2,1,0:T(8,128)S(1)} %copy.25.refs_4_, ...), custom_call_target="tpu_custom_call" | custom-call | flops 1000000000 | bytes 1048576 | tf_op jit(solution)/shard_map/pallas_call | solution.py:118
  50.0 0.0 collective-permute-done.4
  50.0 0.0 collective-permute-done.5
  50.0 0.0 collective-permute-done.6
  50.0 1.7 %collective-permute-done.7.refs_5_ = f32[3,16,8,256]{3,2,1,0:T(8,128)S(1)} collective-permute-done((f32[3,16,8,256]{3,2,1,0:T(8,128)S(1)}, f32[3,16,8,256]{3,2,1,0:T(8,128)S(1)}, u32[]{:S(2)}, u32[]{:S(2)}) %collective-permute-start.7) | collective-permute-done | bytes 393248 | tf_op jit(solution)/shard_map/ppermute | solution.py:148
  51.8 1.5 %collective-permute-start.10 = (f32[3,16,8,256]{3,2,1,0:T(8,128)S(1)}, f32[3,16,8,256]{3,2,1,0:T(8,128)S(1)}, u32[]{:S(2)}, u32[]{:S(2)}) collective-permute-start(f32[3,16,8,256]{3,2,1,0:T(8,128)S(1)} %constant_dynamic-update-slice_fusion.refs_3_), channel_id=1, source_target_pairs={{0,1},{1,0},{2,3},{3,2},{4,5},{5,4},{6,7},{7,6},{8,9},{9,8},{10,11... | collective-permute-start | bytes 1179656 | tf_op jit(solution)/shard_map/ppermute | solution.py:140
  53.3 0.1 collective-permute-start.11
  53.4 0.0 copy-start
  53.4 1.2 %collective-permute-done.10.refs_4_ = f32[3,16,8,256]{3,2,1,0:T(8,128)S(1)} collective-permute-done((f32[3,16,8,256]{3,2,1,0:T(8,128)S(1)}, f32[3,16,8,256]{3,2,1,0:T(8,128)S(1)}, u32[]{:S(2)}, u32[]{:S(2)}) %collective-permute-start.10) | collective-permute-done | bytes 393248 | tf_op jit(solution)/shard_map/ppermute | solution.py:140
  54.7 0.6 collective-permute-done.11.refs_6_
  55.2 4.7 %shard_map.83 = (f32[16,2,8,256]{3,2,1,0:T(8,128)S(1)}, f32[16,2,8,256]{3,2,1,0:T(8,128)S(1)}) custom-call(s32[2,16]{1,0:T(2,128)S(1)} %minimum_bitcast_fusion.refs_0_, s32[1,3,1,8]{3,2,1,0:T(1,128)S(1)} %add_bitcast_fusion.refs_1_, f32[1,3,1,8]{3,2,1,0:T(1,128)S(1)} %fusion.1.refs_2_, f32[3,16,8,256]{3,2,1,0:T(8,128)S(1)} %constant_dynamic-update-slice_fusion.refs_3_, ...), custom_call_target="tpu_custom_call" | custom-call | flops 20000000000 | bytes 1048576 | tf_op jit(solution)/shard_map/pallas_call | solution.py:118
  59.9 0.5 collective-permute-start.12
  60.4 0.0 copy-done
  60.4 0.1 constant_dynamic-slice_fusion
  60.5 1.1 %collective-permute-done.12 = f32[16,2,8,256]{3,2,1,0:T(8,128)S(1)} collective-permute-done((f32[16,2,8,256]{3,2,1,0:T(8,128)S(1)}, f32[16,2,8,256]{3,2,1,0:T(8,128)S(1)}, u32[]{:S(2)}, u32[]{:S(2)}) %collective-permute-start.12) | collective-permute-done | bytes 262176 | tf_op jit(solution)/shard_map/ppermute | solution.py:140
  61.5 0.7 add.35
  62.3 4.8 %all-to-all-start.1 = ((f32[16,2,8,256]{3,2,1,0:T(8,128)}), f32[16,2,8,256]{3,2,1,0:T(8,128)S(1)}, u32[]{:S(2)}, u32[]{:S(2)}) async-start(f32[16,2,8,256]{3,2,1,0:T(8,128)} %add.35), calls=%async_computation.1 | async-start | bytes 524288 | tf_op jit(solution)/shard_map/all_to_all | solution.py:192
  67.1 0.1 iota_compare_fusion.1
  67.1 0.1 broadcast_compare_fusion
  67.2 8.8 %all-to-all-done.1 = f32[16,2,8,256]{3,2,1,0:T(8,128)S(1)} async-done(((f32[16,2,8,256]{3,2,1,0:T(8,128)}), f32[16,2,8,256]{3,2,1,0:T(8,128)S(1)}, u32[]{:S(2)}, u32[]{:S(2)}) %all-to-all-start.1) | async-done | bytes 262176 | tf_op jit(solution)/shard_map/all_to_all | solution.py:192
  76.0 0.7 and_select_fusion
  (11 shorter events, 0.2 us)
Async XLA Ops:
  1.4 18.9 %all-to-all-start = ((f32[16,2,8,256]{3,2,1,0:T(8,128)}), f32[16,2,8,256]{3,2,1,0:T(8,128)S(1)}, u32[]{:S(2)}, u32[]{:S(2)}) async-start(f32[16,2,8,256]{3,2,1,0:T(8,128)} %broadcast_in_dim.29), calls=%async_computation | async-start | bytes 524288 | tf_op jit(solution)/shard_map/all_to_all | solution.py:158
  20.3 8.3 %collective-permute-start = (f32[1,16,2,8,256]{4,3,1,0,2:T(8,128)S(1)}, f32[1,16,2,8,256]{4,3,1,0,2:T(8,128)S(1)}, u32[]{:S(2)}, u32[]{:S(2)}) collective-permute-start(f32[1,16,2,8,256]{4,3,1,0,2:T(8,128)S(1)} %bitcast.27), channel_id=1, source_target_pairs={{0,128},{128,0},{1,129},{129,1},{2,130},{130,2},{3,131},{131,3},{4... | collective-permute-start | bytes 786440 | tf_op jit(solution)/shard_map/ppermute | solution.py:148
  23.0 6.7 %collective-permute-start.1 = (f32[1,16,2,8,256]{4,3,1,0,2:T(8,128)S(1)}, f32[1,16,2,8,256]{4,3,1,0,2:T(8,128)S(1)}, u32[]{:S(2)}, u32[]{:S(2)}) collective-permute-start(f32[1,16,2,8,256]{4,3,1,0,2:T(8,128)S(1)} %bitcast.28), channel_id=1, source_target_pairs={{0,32},{32,64},{64,96},{96,0},{1,33},{33,65},{65,97},{97,1},{2,34}... | collective-permute-start | bytes 786440 | tf_op jit(solution)/shard_map/ppermute | solution.py:144
  24.3 5.5 %collective-permute-start.2 = (f32[1,16,2,8,256]{4,3,1,0,2:T(8,128)S(1)}, f32[1,16,2,8,256]{4,3,1,0,2:T(8,128)S(1)}, u32[]{:S(2)}, u32[]{:S(2)}) collective-permute-start(f32[1,16,2,8,256]{4,3,1,0,2:T(8,128)S(1)} %bitcast.29), channel_id=1, source_target_pairs={{0,96},{32,0},{64,32},{96,64},{1,97},{33,1},{65,33},{97,65},{2,98}... | collective-permute-start | bytes 786440 | tf_op jit(solution)/shard_map/ppermute | solution.py:144
  25.7 10.0 %collective-permute-start.3 = (f32[1,16,2,8,256]{4,3,1,0,2:T(8,128)S(1)}, f32[1,16,2,8,256]{4,3,1,0,2:T(8,128)S(1)}, u32[]{:S(2)}, u32[]{:S(2)}) collective-permute-start(f32[1,16,2,8,256]{4,3,1,0,2:T(8,128)S(1)} %bitcast.30), channel_id=1, source_target_pairs={{0,64},{32,96},{64,0},{96,32},{1,65},{33,97},{65,1},{97,33},{2,66}... | collective-permute-start | bytes 786440 | tf_op jit(solution)/shard_map/ppermute | solution.py:144
  35.8 7.7 %collective-permute-start.8 = (f32[4,16,2,8,256]{4,3,1,0,2:T(8,128)S(1)}, f32[4,16,2,8,256]{4,3,1,0,2:T(8,128)S(1)}, u32[]{:S(2)}, u32[]{:S(2)}) collective-permute-start(f32[4,16,2,8,256]{4,3,1,0,2:T(8,128)S(1)} %pad_maximum_fusion), channel_id=1, source_target_pairs={{0,1},{1,0},{2,3},{3,2},{4,5},{5,4},{6,7},{7,6},{8,9},{9,8},{10,11... | collective-permute-start | bytes 3145736 | tf_op jit(solution)/shard_map/ppermute | solution.py:140
  39.7 3.3 %collective-permute-start.9 = (f32[1,16,2,8,256]{4,3,1,0,2:T(8,128)S(1)}, f32[1,16,2,8,256]{4,3,1,0,2:T(8,128)S(1)}, u32[]{:S(2)}, u32[]{:S(2)}) collective-permute-start(f32[1,16,2,8,256]{4,3,1,0,2:T(8,128)S(1)} %collective-permute-done), channel_id=1, source_target_pairs={{0,1},{1,0},{2,3},{3,2},{4,5},{5,4},{6,7},{7,6},{8,9},{9,8},{10,11... | collective-permute-start | bytes 786440 | tf_op jit(solution)/shard_map/ppermute | solution.py:140
  39.9 11.9 %collective-permute-start.7 = (f32[3,16,8,256]{3,2,1,0:T(8,128)S(1)}, f32[3,16,8,256]{3,2,1,0:T(8,128)S(1)}, u32[]{:S(2)}, u32[]{:S(2)}) collective-permute-start(f32[3,16,8,256]{3,2,1,0:T(8,128)S(1)} %fusion), channel_id=1, source_target_pairs={{0,128},{128,0},{1,129},{129,1},{2,130},{130,2},{3,131},{131,3},{4... | collective-permute-start | bytes 1179656 | tf_op jit(solution)/shard_map/ppermute | solution.py:148
  40.3 9.7 %collective-permute-start.4 = (f32[1,16,8,256]{3,2,1,0:T(8,128)S(1)}, f32[1,16,8,256]{3,2,1,0:T(8,128)S(1)}, u32[]{:S(2)}, u32[]{:S(2)}) collective-permute-start(f32[1,16,8,256]{3,2,1,0:T(8,128)S(1)} %slice_bitcast_fusion), channel_id=1, source_target_pairs={{0,32},{32,64},{64,96},{96,0},{1,33},{33,65},{65,97},{97,1},{2,34}... | collective-permute-start | bytes 393224 | tf_op jit(solution)/shard_map/ppermute | solution.py:144
  41.3 8.7 %collective-permute-start.5 = (f32[1,16,8,256]{3,2,1,0:T(8,128)S(1)}, f32[1,16,8,256]{3,2,1,0:T(8,128)S(1)}, u32[]{:S(2)}, u32[]{:S(2)}) collective-permute-start(f32[1,16,8,256]{3,2,1,0:T(8,128)S(1)} %slice_bitcast_fusion), channel_id=1, source_target_pairs={{0,96},{32,0},{64,32},{96,64},{1,97},{33,1},{65,33},{97,65},{2,98}... | collective-permute-start | bytes 393224 | tf_op jit(solution)/shard_map/ppermute | solution.py:144
  43.1 6.9 %collective-permute-start.6 = (f32[1,16,8,256]{3,2,1,0:T(8,128)S(1)}, f32[1,16,8,256]{3,2,1,0:T(8,128)S(1)}, u32[]{:S(2)}, u32[]{:S(2)}) collective-permute-start(f32[1,16,8,256]{3,2,1,0:T(8,128)S(1)} %slice_bitcast_fusion), channel_id=1, source_target_pairs={{0,64},{32,96},{64,0},{96,32},{1,65},{33,97},{65,1},{97,33},{2,66}... | collective-permute-start | bytes 393224 | tf_op jit(solution)/shard_map/ppermute | solution.py:144
  51.8 2.9 %collective-permute-start.10 = (f32[3,16,8,256]{3,2,1,0:T(8,128)S(1)}, f32[3,16,8,256]{3,2,1,0:T(8,128)S(1)}, u32[]{:S(2)}, u32[]{:S(2)}) collective-permute-start(f32[3,16,8,256]{3,2,1,0:T(8,128)S(1)} %constant_dynamic-update-slice_fusion.refs_3_), channel_id=1, source_target_pairs={{0,1},{1,0},{2,3},{3,2},{4,5},{5,4},{6,7},{7,6},{8,9},{9,8},{10,11... | collective-permute-start | bytes 1179656 | tf_op jit(solution)/shard_map/ppermute | solution.py:140
  53.3 1.9 %collective-permute-start.11 = (f32[3,16,8,256]{3,2,1,0:T(8,128)S(1)}, f32[3,16,8,256]{3,2,1,0:T(8,128)S(1)}, u32[]{:S(2)}, u32[]{:S(2)}) collective-permute-start(f32[3,16,8,256]{3,2,1,0:T(8,128)S(1)} %collective-permute-done.7.refs_5_), channel_id=1, source_target_pairs={{0,1},{1,0},{2,3},{3,2},{4,5},{5,4},{6,7},{7,6},{8,9},{9,8},{10,11... | collective-permute-start | bytes 1179656 | tf_op jit(solution)/shard_map/ppermute | solution.py:140
  53.4 7.0 %copy-start = (s32[16,2]{0,1:T(2,128)S(1)}, s32[16,2]{0,1:T(2,128)}, u32[]{:S(2)}) copy-start(s32[16,2]{0,1:T(2,128)} %param.9) | copy-start | bytes 388
  59.9 1.6 %collective-permute-start.12 = (f32[16,2,8,256]{3,2,1,0:T(8,128)S(1)}, f32[16,2,8,256]{3,2,1,0:T(8,128)S(1)}, u32[]{:S(2)}, u32[]{:S(2)}) collective-permute-start(f32[16,2,8,256]{3,2,1,0:T(8,128)S(1)} %get-tuple-element.32), channel_id=1, source_target_pairs={{0,1},{1,0},{2,3},{3,2},{4,5},{5,4},{6,7},{7,6},{8,9},{9,8},{10,11... | collective-permute-start | bytes 786440 | tf_op jit(solution)/shard_map/ppermute | solution.py:140
  62.3 13.7 %all-to-all-start.1 = ((f32[16,2,8,256]{3,2,1,0:T(8,128)}), f32[16,2,8,256]{3,2,1,0:T(8,128)S(1)}, u32[]{:S(2)}, u32[]{:S(2)}) async-start(f32[16,2,8,256]{3,2,1,0:T(8,128)} %add.35), calls=%async_computation.1 | async-start | bytes 524288 | tf_op jit(solution)/shard_map/all_to_all | solution.py:192

commit v4 on v3

--- a/solution.py
+++ b/solution.py
@@ -168,25 +168,23 @@
         *[lax.transpose(array, (0, 3, 1, 2)) for array in (codes, scales)],
     )
     (crossed, *beside), lists = lax.optimization_barrier(
-        ([across(runs), *[ahead(runs, step) for step in STEPS[1:]]], lists)
-    )
-    near = jnp.concatenate([runs, *beside])
-    far_first = [ahead(crossed[:, :, 0], step) for step in STEPS[1:]]
-    far_second = across(near[1:, :, 1])
-
-    near_other, crossed_other = swap_core(near), swap_core(crossed)
-    parts = [(0, 0), (1, 0), (0, 1), (0, 2), (0, 3)]
+        ([across(runs), *[ahead(runs, step) for step in STEPS[1:3]]], lists)
+    )
+    column, row = jnp.concatenate([runs, crossed]), jnp.concatenate(beside)
+    far_row, far_column = across(row), ahead(column, STEPS[3])
+
+    near = [runs, crossed, *beside]
     panels = []
-    for side, k in parts:
-        both = (near, near_other) if side == 0 else (crossed, crossed_other)
-        panels += [(array, k, True) for array in both] * 2
-    sums = chunk(parts, lists, panels, left, right, None)
-
-    far_first, far_second, sums = lax.optimization_barrier((far_first, far_second, sums))
-    far_first = jnp.concatenate(far_first)
-    far = (far_first, swap_core(far_first), far_second, swap_core(far_second))
-    parts = [(1, 1), (1, 2), (1, 3)]
-    panels = [(array, k - 1, False) for _, k in parts for array in far]
+    for piece in near:
+        other = swap_core(piece)
+        panels += [(array, 0, True) for array in (piece, other)] * 2
+    sums = chunk([(0, 0), (1, 0), (0, 1), (0, 2)], lists, panels, left, right, None)
+
+    far_row, far_column, sums = lax.optimization_barrier((far_row, far_column, sums))
+    row, column = (far_row, swap_core(far_row)), (far_column, swap_core(far_column))
+    places = [(row, 0), (row, 1), (column, 0), (column, 1)]
+    panels = [(array, at, True) for held, at in places for array in held * 2]
+    parts = [(1, 1), (1, 2), (0, 3), (1, 3)]
     keep, give = chunk(parts, lists, panels, left, right, sums)
     half = keep + swap_core(give)
     summed = lax.all_to_all(half, ("y_lo", "z"), 0, 0).sum(0)

time: 77.9 us -> 73.3 us (0.941)
  waiting for transfers between devices: 27.1 us -> 20.1 us
  starting transfers between devices: 31.3 us -> 34.2 us
    ppermute x6 -> x3, waiting for transfers between devices: 7.11 us -> 0.01 us  [ahead(): return lax.ppermute(value, 'x', [(x, (x + step) % 4) for x in range(4)])]
    ppermute x5 -> x7, starting transfers between devices: 6.1 us -> 10.7 us  [swap_core(): return lax.ppermute(value, 'core', [(0, 1), (1, 0)])]
    ppermute x6 -> x3, starting transfers between devices: 7.17 us -> 4.68 us  [ahead(): return lax.ppermute(value, 'x', [(x, (x + step) % 4) for x in range(4)])]
    ppermute x5 -> x7, waiting for transfers between devices: 2.9 us -> 4.76 us  [swap_core(): return lax.ppermute(value, 'core', [(0, 1), (1, 0)])]
    ppermute x2, waiting for transfers between devices: 1.75 us -> 0.01 us  [across(): return lax.ppermute(value, 'y_hi', [(0, 1), (1, 0)])]
    all_to_all x1, starting transfers between devices: 4.77 us -> 5.66 us  [local(): summed = lax.all_to_all(half, ('y_lo', 'z'), 0, 0).sum(0)]
  transfers between devices with their start and end apart: 15 -> 14, of which waited for: 8 -> 8; matrix products, arithmetic and copies ran while one was open for 5% -> 5% of each run, Pallas kernels for 8% -> 8%
where the time goes in v4:
time: 73.3 us; the launch traced here: 72.1 us
  starting transfers between devices  34.2 us (47%)
  waiting for transfers between devices  20.1 us (27%)
  Pallas kernels  11 us (15%)
  other arithmetic  4.53 us (6%)
  local copies, waits for them, and re-layouts  2.2 us (3%)
    pallas_call x2, Pallas kernels, chunk(): pl.pallas_call(kernel, in_specs=[smem] * 3 + [vmem] * len(arrays) + [hbm]...  11 us
    ppermute x7, starting transfers between devices, swap_core(): return lax.ppermute(value, 'core', [(0, 1), (1, 0)])  10.7 us
    all_to_all x1, starting transfers between devices, local(): lax.all_to_all(jnp.broadcast_to(wavefunction[None], (RUNS,) + wavefunctio...  10.1 us
    all_to_all x1, waiting for transfers between devices, local(): summed = lax.all_to_all(half, ('y_lo', 'z'), 0, 0).sum(0)  8.78 us
    all_to_all x1, waiting for transfers between devices, local(): lax.all_to_all(jnp.broadcast_to(wavefunction[None], (RUNS,) + wavefunctio...  6.55 us
    all_to_all x1, starting transfers between devices, local(): summed = lax.all_to_all(half, ('y_lo', 'z'), 0, 0).sum(0)  5.66 us
    ppermute x7, waiting for transfers between devices, swap_core(): return lax.ppermute(value, 'core', [(0, 1), (1, 0)])  4.76 us
    ppermute x3, starting transfers between devices, ahead(): return lax.ppermute(value, 'x', [(x, (x + step) % 4) for x in range(4)])  4.68 us
  transfers between devices with their start and end apart: 14, of which 8 were waited for; matrix products, arithmetic and copies ran while one was open for 5% of the time, Pallas kernels for 8%

profile of v4, /device:TPU:1, one launch (start us, length us, event | category | flops | bytes accessed | tf_op | source)
XLA Modules:
  0.0 72.1 jit_solution(229846529479122079)
XLA Ops:
  0.0 1.4 %broadcast_in_dim.29 = f32[16,2,8,256]{3,2,1,0:T(8,128)} broadcast(f32[2,8,256]{2,1,0:T(8,128)} %param.8), dimensions={1,2,3} | broadcast | bytes 278528 | tf_op jit(solution)/shard_map/broadcast_in_dim | solution.py:159
  1.4 10.1 %all-to-all-start = ((f32[16,2,8,256]{3,2,1,0:T(8,128)}), f32[16,2,8,256]{3,2,1,0:T(8,128)S(1)}, u32[]{:S(2)}, u32[]{:S(2)}) async-start(f32[16,2,8,256]{3,2,1,0:T(8,128)} %broadcast_in_dim.29), calls=%async_computation | async-start | bytes 524288 | tf_op jit(solution)/shard_map/all_to_all | solution.py:158
  11.6 0.7 copy.15
  12.3 0.8 %select_reduce_fusion = f32[8,3]{0,1:T(4,128)S(1)} fusion(f32[26]{0:T(128)} %param.12, s32[8,3]{0,1:T(4,128)S(1)} %bitcast.27), kind=kLoop, calls=%fused_computation.3 | loop fusion | flops 1848 | bytes 296 | tf_op jit(solution)/shard_map/reduce_sum | solution.py:164
  13.1 0.7 fusion.refs_2_
  13.8 6.5 %all-to-all-done = f32[16,2,8,256]{3,2,1,0:T(8,128)S(1)} async-done(((f32[16,2,8,256]{3,2,1,0:T(8,128)}), f32[16,2,8,256]{3,2,1,0:T(8,128)S(1)}, u32[]{:S(2)}, u32[]{:S(2)}) %all-to-all-start) | async-done | bytes 262176 | tf_op jit(solution)/shard_map/all_to_all | solution.py:158
  20.3 2.6 %collective-permute-start = (f32[1,16,2,8,256]{4,3,2,1,0:T(8,128)S(1)}, f32[1,16,2,8,256]{4,3,2,1,0:T(8,128)S(1)}, u32[]{:S(2)}, u32[]{:S(2)}) collective-permute-start(f32[1,16,2,8,256]{4,3,2,1,0:T(8,128)S(1)} %bitcast.17), channel_id=1, source_target_pairs={{0,128},{128,0},{1,129},{129,1},{2,130},{130,2},{3,131},{131,3},{4... | collective-permute-start | bytes 786440 | tf_op jit(solution)/shard_map/ppermute | solution.py:148
  22.9 1.2 %collective-permute-start.1 = (f32[1,16,2,8,256]{4,3,2,1,0:T(8,128)S(1)}, f32[1,16,2,8,256]{4,3,2,1,0:T(8,128)S(1)}, u32[]{:S(2)}, u32[]{:S(2)}) collective-permute-start(f32[1,16,2,8,256]{4,3,2,1,0:T(8,128)S(1)} %bitcast.18), channel_id=1, source_target_pairs={{0,32},{32,64},{64,96},{96,0},{1,33},{33,65},{65,97},{97,1},{2,34}... | collective-permute-start | bytes 786440 | tf_op jit(solution)/shard_map/ppermute | solution.py:144
  24.1 1.5 %collective-permute-start.2 = (f32[1,16,2,8,256]{4,3,2,1,0:T(8,128)S(1)}, f32[1,16,2,8,256]{4,3,2,1,0:T(8,128)S(1)}, u32[]{:S(2)}, u32[]{:S(2)}) collective-permute-start(f32[1,16,2,8,256]{4,3,2,1,0:T(8,128)S(1)} %bitcast.19), channel_id=1, source_target_pairs={{0,96},{32,0},{64,32},{96,64},{1,97},{33,1},{65,33},{97,65},{2,98}... | collective-permute-start | bytes 786440 | tf_op jit(solution)/shard_map/ppermute | solution.py:144
  25.6 0.7 minimum_bitcast_fusion.refs_0_
  26.3 0.7 add_bitcast_fusion.refs_1_
  27.0 3.2 %collective-permute-start.5 = (f32[1,16,2,8,256]{4,3,2,1,0:T(8,128)S(1)}, f32[1,16,2,8,256]{4,3,2,1,0:T(8,128)S(1)}, u32[]{:S(2)}, u32[]{:S(2)}) collective-permute-start(f32[1,16,2,8,256]{4,3,2,1,0:T(8,128)S(1)} %bitcast.20), channel_id=1, source_target_pairs={{0,1},{1,0},{2,3},{3,2},{4,5},{5,4},{6,7},{7,6},{8,9},{9,8},{10,11... | collective-permute-start | bytes 786440 | tf_op jit(solution)/shard_map/ppermute | solution.py:140
  30.2 0.0 collective-permute-done.refs_5_
  30.2 0.0 collective-permute-done.1.refs_7_
  30.2 0.0 collective-permute-done.2.refs_9_
  30.2 0.4 collective-permute-start.3
  30.7 2.0 %collective-permute-start.4 = (f32[2,16,2,8,256]{4,3,2,1,0:T(8,128)S(1)}, f32[2,16,2,8,256]{4,3,2,1,0:T(8,128)S(1)}, u32[]{:S(2)}, u32[]{:S(2)}) collective-permute-start(f32[2,16,2,8,256]{4,3,2,1,0:T(8,128)S(1)} %pad_maximum_fusion.1), channel_id=1, source_target_pairs={{0,64},{32,96},{64,0},{96,32},{1,65},{33,97},{65,1},{97,33},{2,66}... | collective-permute-start | bytes 1572872 | tf_op jit(solution)/shard_map/ppermute | solution.py:144
  32.7 4.3 %collective-permute-start.6 = (f32[1,16,2,8,256]{4,3,2,1,0:T(8,128)S(1)}, f32[1,16,2,8,256]{4,3,2,1,0:T(8,128)S(1)}, u32[]{:S(2)}, u32[]{:S(2)}) collective-permute-start(f32[1,16,2,8,256]{4,3,2,1,0:T(8,128)S(1)} %collective-permute-done.refs_5_), channel_id=1, source_target_pairs={{0,1},{1,0},{2,3},{3,2},{4,5},{5,4},{6,7},{7,6},{8,9},{9,8},{10,11... | collective-permute-start | bytes 786440 | tf_op jit(solution)/shard_map/ppermute | solution.py:140
  37.0 0.0 collective-permute-start.7
  37.0 0.0 collective-permute-done.5.refs_4_
  37.0 0.5 collective-permute-start.8
  37.5 0.6 collective-permute-done.6.refs_6_
  38.2 0.4 collective-permute-done.7.refs_8_
  38.6 0.4 collective-permute-done.8.refs_10_
  38.9 5.4 %shard_map.82.refs_9_ = f32[2,256,256]{2,1,0:T(8,128)S(1)} custom-call(s32[2,16]{1,0:T(2,128)S(1)} %minimum_bitcast_fusion.refs_0_, s32[1,3,1,8]{3,2,1,0:T(1,128)S(1)} %add_bitcast_fusion.refs_1_, f32[1,3,1,8]{3,2,1,0:T(1,128)S(1)} %fusion.refs_2_, f32[1,16,2,8,256]{4,3,2,1,0:T(8,128)S(1)} %bitcast.22, ...), custom_call_target="tpu_custom_call" | custom-call | flops 1000000000 | bytes 1048576 | tf_op jit(solution)/shard_map/pallas_call | solution.py:118
  44.4 0.0 collective-permute-done.3.refs_3_
  44.4 0.0 collective-permute-done.4.refs_5_
  44.4 2.2 %collective-permute-start.10 = (f32[2,16,2,8,256]{4,3,2,1,0:T(8,128)S(1)}, f32[2,16,2,8,256]{4,3,2,1,0:T(8,128)S(1)}, u32[]{:S(2)}, u32[]{:S(2)}) collective-permute-start(f32[2,16,2,8,256]{4,3,2,1,0:T(8,128)S(1)} %collective-permute-done.4.refs_5_), channel_id=1, source_target_pairs={{0,1},{1,0},{2,3},{3,2},{4,5},{5,4},{6,7},{7,6},{8,9},{9,8},{10,11... | collective-permute-start | bytes 1572872 | tf_op jit(solution)/shard_map/ppermute | solution.py:140
  46.6 0.0 collective-permute-start.9
  46.6 0.0 copy-start
  46.6 1.5 %collective-permute-done.10.refs_6_ = f32[2,16,2,8,256]{4,3,2,1,0:T(8,128)S(1)} collective-permute-done((f32[2,16,2,8,256]{4,3,2,1,0:T(8,128)S(1)}, f32[2,16,2,8,256]{4,3,2,1,0:T(8,128)S(1)}, u32[]{:S(2)}, u32[]{:S(2)}) %collective-permute-start.10) | collective-permute-done | bytes 524320 | tf_op jit(solution)/shard_map/ppermute | solution.py:140
  48.2 0.7 %collective-permute-done.9.refs_4_ = f32[2,16,2,8,256]{4,3,2,1,0:T(8,128)S(1)} collective-permute-done((f32[2,16,2,8,256]{4,3,2,1,0:T(8,128)S(1)}, f32[2,16,2,8,256]{4,3,2,1,0:T(8,128)S(1)}, u32[]{:S(2)}, u32[]{:S(2)}) %collective-permute-start.9) | collective-permute-done | bytes 524320 | tf_op jit(solution)/shard_map/ppermute | solution.py:140
  48.9 5.5 %shard_map.83 = (f32[16,2,8,256]{3,2,1,0:T(8,128)S(1)}, f32[16,2,8,256]{3,2,1,0:T(8,128)S(1)}) custom-call(s32[2,16]{1,0:T(2,128)S(1)} %minimum_bitcast_fusion.refs_0_, s32[1,3,1,8]{3,2,1,0:T(1,128)S(1)} %add_bitcast_fusion.refs_1_, f32[1,3,1,8]{3,2,1,0:T(1,128)S(1)} %fusion.refs_2_, f32[2,16,2,8,256]{4,3,2,1,0:T(8,128)S(1)} %collective-permute-done.3.refs_3_, ...), custom_call_target="tpu_custom_call" | custom-call | flops 20000000000 | bytes 1048576 | tf_op jit(solution)/shard_map/pallas_call | solution.py:118
  54.5 0.5 collective-permute-start.11
  54.9 0.0 copy-done
  54.9 0.1 constant_dynamic-slice_fusion
  55.0 1.1 %collective-permute-done.11 = f32[16,2,8,256]{3,2,1,0:T(8,128)S(1)} collective-permute-done((f32[16,2,8,256]{3,2,1,0:T(8,128)S(1)}, f32[16,2,8,256]{3,2,1,0:T(8,128)S(1)}, u32[]{:S(2)}, u32[]{:S(2)}) %collective-permute-start.11) | collective-permute-done | bytes 262176 | tf_op jit(solution)/shard_map/ppermute | solution.py:140
  56.1 0.7 %add.35 = f32[16,2,8,256]{3,2,1,0:T(8,128)} add(f32[16,2,8,256]{3,2,1,0:T(8,128)S(1)} %get-tuple-element.25, f32[16,2,8,256]{3,2,1,0:T(8,128)S(1)} %collective-permute-done.11) | non-fusion elementwise | flops 65536 | bytes 786432 | tf_op jit(solution)/shard_map/add | solution.py:189
  56.8 5.7 %all-to-all-start.1 = ((f32[16,2,8,256]{3,2,1,0:T(8,128)}), f32[16,2,8,256]{3,2,1,0:T(8,128)S(1)}, u32[]{:S(2)}, u32[]{:S(2)}) async-start(f32[16,2,8,256]{3,2,1,0:T(8,128)} %add.35), calls=%async_computation.1 | async-start | bytes 524288 | tf_op jit(solution)/shard_map/all_to_all | solution.py:190
  62.5 0.1 iota_compare_fusion.1
  62.6 0.1 broadcast_compare_fusion
  62.6 8.8 %all-to-all-done.1 = f32[16,2,8,256]{3,2,1,0:T(8,128)S(1)} async-done(((f32[16,2,8,256]{3,2,1,0:T(8,128)}), f32[16,2,8,256]{3,2,1,0:T(8,128)S(1)}, u32[]{:S(2)}, u32[]{:S(2)}) %all-to-all-start.1) | async-done | bytes 262176 | tf_op jit(solution)/shard_map/all_to_all | solution.py:190
  71.5 0.7 and_select_fusion
  (5 shorter events, 0.1 us)
Async XLA Ops:
  1.4 18.9 %all-to-all-start = ((f32[16,2,8,256]{3,2,1,0:T(8,128)}), f32[16,2,8,256]{3,2,1,0:T(8,128)S(1)}, u32[]{:S(2)}, u32[]{:S(2)}) async-start(f32[16,2,8,256]{3,2,1,0:T(8,128)} %broadcast_in_dim.29), calls=%async_computation | async-start | bytes 524288 | tf_op jit(solution)/shard_map/all_to_all | solution.py:158
  20.3 9.9 %collective-permute-start = (f32[1,16,2,8,256]{4,3,2,1,0:T(8,128)S(1)}, f32[1,16,2,8,256]{4,3,2,1,0:T(8,128)S(1)}, u32[]{:S(2)}, u32[]{:S(2)}) collective-permute-start(f32[1,16,2,8,256]{4,3,2,1,0:T(8,128)S(1)} %bitcast.17), channel_id=1, source_target_pairs={{0,128},{128,0},{1,129},{129,1},{2,130},{130,2},{3,131},{131,3},{4... | collective-permute-start | bytes 786440 | tf_op jit(solution)/shard_map/ppermute | solution.py:148
  22.9 7.2 %collective-permute-start.1 = (f32[1,16,2,8,256]{4,3,2,1,0:T(8,128)S(1)}, f32[1,16,2,8,256]{4,3,2,1,0:T(8,128)S(1)}, u32[]{:S(2)}, u32[]{:S(2)}) collective-permute-start(f32[1,16,2,8,256]{4,3,2,1,0:T(8,128)S(1)} %bitcast.18), channel_id=1, source_target_pairs={{0,32},{32,64},{64,96},{96,0},{1,33},{33,65},{65,97},{97,1},{2,34}... | collective-permute-start | bytes 786440 | tf_op jit(solution)/shard_map/ppermute | solution.py:144
  24.1 6.0 %collective-permute-start.2 = (f32[1,16,2,8,256]{4,3,2,1,0:T(8,128)S(1)}, f32[1,16,2,8,256]{4,3,2,1,0:T(8,128)S(1)}, u32[]{:S(2)}, u32[]{:S(2)}) collective-permute-start(f32[1,16,2,8,256]{4,3,2,1,0:T(8,128)S(1)} %bitcast.19), channel_id=1, source_target_pairs={{0,96},{32,0},{64,32},{96,64},{1,97},{33,1},{65,33},{97,65},{2,98}... | collective-permute-start | bytes 786440 | tf_op jit(solution)/shard_map/ppermute | solution.py:144
  27.0 10.0 %collective-permute-start.5 = (f32[1,16,2,8,256]{4,3,2,1,0:T(8,128)S(1)}, f32[1,16,2,8,256]{4,3,2,1,0:T(8,128)S(1)}, u32[]{:S(2)}, u32[]{:S(2)}) collective-permute-start(f32[1,16,2,8,256]{4,3,2,1,0:T(8,128)S(1)} %bitcast.20), channel_id=1, source_target_pairs={{0,1},{1,0},{2,3},{3,2},{4,5},{5,4},{6,7},{7,6},{8,9},{9,8},{10,11... | collective-permute-start | bytes 786440 | tf_op jit(solution)/shard_map/ppermute | solution.py:140
  30.2 14.2 %collective-permute-start.3 = (f32[2,16,2,8,256]{4,3,2,1,0:T(8,128)S(1)}, f32[2,16,2,8,256]{4,3,2,1,0:T(8,128)S(1)}, u32[]{:S(2)}, u32[]{:S(2)}) collective-permute-start(f32[2,16,2,8,256]{4,3,2,1,0:T(8,128)S(1)} %pad_maximum_fusion), channel_id=1, source_target_pairs={{0,128},{128,0},{1,129},{129,1},{2,130},{130,2},{3,131},{131,3},{4... | collective-permute-start | bytes 1572872 | tf_op jit(solution)/shard_map/ppermute | solution.py:148
  30.7 13.7 %collective-permute-start.4 = (f32[2,16,2,8,256]{4,3,2,1,0:T(8,128)S(1)}, f32[2,16,2,8,256]{4,3,2,1,0:T(8,128)S(1)}, u32[]{:S(2)}, u32[]{:S(2)}) collective-permute-start(f32[2,16,2,8,256]{4,3,2,1,0:T(8,128)S(1)} %pad_maximum_fusion.1), channel_id=1, source_target_pairs={{0,64},{32,96},{64,0},{96,32},{1,65},{33,97},{65,1},{97,33},{2,66}... | collective-permute-start | bytes 1572872 | tf_op jit(solution)/shard_map/ppermute | solution.py:144
  32.7 5.5 %collective-permute-start.6 = (f32[1,16,2,8,256]{4,3,2,1,0:T(8,128)S(1)}, f32[1,16,2,8,256]{4,3,2,1,0:T(8,128)S(1)}, u32[]{:S(2)}, u32[]{:S(2)}) collective-permute-start(f32[1,16,2,8,256]{4,3,2,1,0:T(8,128)S(1)} %collective-permute-done.refs_5_), channel_id=1, source_target_pairs={{0,1},{1,0},{2,3},{3,2},{4,5},{5,4},{6,7},{7,6},{8,9},{9,8},{10,11... | collective-permute-start | bytes 786440 | tf_op jit(solution)/shard_map/ppermute | solution.py:140
  37.0 1.5 %collective-permute-start.7 = (f32[1,16,2,8,256]{4,3,2,1,0:T(8,128)S(1)}, f32[1,16,2,8,256]{4,3,2,1,0:T(8,128)S(1)}, u32[]{:S(2)}, u32[]{:S(2)}) collective-permute-start(f32[1,16,2,8,256]{4,3,2,1,0:T(8,128)S(1)} %collective-permute-done.1.refs_7_), channel_id=1, source_target_pairs={{0,1},{1,0},{2,3},{3,2},{4,5},{5,4},{6,7},{7,6},{8,9},{9,8},{10,11... | collective-permute-start | bytes 786440 | tf_op jit(solution)/shard_map/ppermute | solution.py:140
  37.0 1.9 %collective-permute-start.8 = (f32[1,16,2,8,256]{4,3,2,1,0:T(8,128)S(1)}, f32[1,16,2,8,256]{4,3,2,1,0:T(8,128)S(1)}, u32[]{:S(2)}, u32[]{:S(2)}) collective-permute-start(f32[1,16,2,8,256]{4,3,2,1,0:T(8,128)S(1)} %collective-permute-done.2.refs_9_), channel_id=1, source_target_pairs={{0,1},{1,0},{2,3},{3,2},{4,5},{5,4},{6,7},{7,6},{8,9},{9,8},{10,11... | collective-permute-start | bytes 786440 | tf_op jit(solution)/shard_map/ppermute | solution.py:140
  44.4 3.8 %collective-permute-start.10 = (f32[2,16,2,8,256]{4,3,2,1,0:T(8,128)S(1)}, f32[2,16,2,8,256]{4,3,2,1,0:T(8,128)S(1)}, u32[]{:S(2)}, u32[]{:S(2)}) collective-permute-start(f32[2,16,2,8,256]{4,3,2,1,0:T(8,128)S(1)} %collective-permute-done.4.refs_5_), channel_id=1, source_target_pairs={{0,1},{1,0},{2,3},{3,2},{4,5},{5,4},{6,7},{7,6},{8,9},{9,8},{10,11... | collective-permute-start | bytes 1572872 | tf_op jit(solution)/shard_map/ppermute | solution.py:140
  46.6 2.3 %collective-permute-start.9 = (f32[2,16,2,8,256]{4,3,2,1,0:T(8,128)S(1)}, f32[2,16,2,8,256]{4,3,2,1,0:T(8,128)S(1)}, u32[]{:S(2)}, u32[]{:S(2)}) collective-permute-start(f32[2,16,2,8,256]{4,3,2,1,0:T(8,128)S(1)} %collective-permute-done.3.refs_3_), channel_id=1, source_target_pairs={{0,1},{1,0},{2,3},{3,2},{4,5},{5,4},{6,7},{7,6},{8,9},{9,8},{10,11... | collective-permute-start | bytes 1572872 | tf_op jit(solution)/shard_map/ppermute | solution.py:140
  46.6 8.3 %copy-start = (s32[16,2]{0,1:T(2,128)S(1)}, s32[16,2]{0,1:T(2,128)}, u32[]{:S(2)}) copy-start(s32[16,2]{0,1:T(2,128)} %param.9) | copy-start | bytes 388
  54.5 1.6 %collective-permute-start.11 = (f32[16,2,8,256]{3,2,1,0:T(8,128)S(1)}, f32[16,2,8,256]{3,2,1,0:T(8,128)S(1)}, u32[]{:S(2)}, u32[]{:S(2)}) collective-permute-start(f32[16,2,8,256]{3,2,1,0:T(8,128)S(1)} %get-tuple-element.26), channel_id=1, source_target_pairs={{0,1},{1,0},{2,3},{3,2},{4,5},{5,4},{6,7},{7,6},{8,9},{9,8},{10,11... | collective-permute-start | bytes 786440 | tf_op jit(solution)/shard_map/ppermute | solution.py:140
  56.8 14.6 %all-to-all-start.1 = ((f32[16,2,8,256]{3,2,1,0:T(8,128)}), f32[16,2,8,256]{3,2,1,0:T(8,128)S(1)}, u32[]{:S(2)}, u32[]{:S(2)}) async-start(f32[16,2,8,256]{3,2,1,0:T(8,128)} %add.35), calls=%async_computation.1 | async-start | bytes 524288 | tf_op jit(solution)/shard_map/all_to_all | solution.py:190

commit v5 on v4

--- a/solution.py
+++ b/solution.py
@@ -159,16 +159,19 @@
         jnp.broadcast_to(wavefunction[None], (RUNS,) + wavefunction.shape), ("y_lo", "z"), 0, 0
     )
     runs = runs[None]
+    (crossed, *beside), (bond_index, in_pair, out_pair, sizes) = lax.optimization_barrier(
+        (
+            [across(runs), *[ahead(runs, step) for step in STEPS[1:3]]],
+            (bond_index, in_pair, out_pair, sector_sizes),
+        )
+    )
     live = out_pair >= 0
     picked = bond_index[..., None] == jnp.arange(mpo_weight.shape[0], dtype=jnp.int32)
     scales = jnp.where(live, jnp.sum(jnp.where(picked, mpo_weight, 0.0), axis=-1), 0.0)
     codes = in_pair * 2 + jnp.maximum(out_pair, 0)
     lists = (
-        jnp.minimum(sector_sizes.T, STATES),
+        jnp.minimum(sizes.T, STATES),
         *[lax.transpose(array, (0, 3, 1, 2)) for array in (codes, scales)],
-    )
-    (crossed, *beside), lists = lax.optimization_barrier(
-        ([across(runs), *[ahead(runs, step) for step in STEPS[1:3]]], lists)
     )
     column, row = jnp.concatenate([runs, crossed]), jnp.concatenate(beside)
     far_row, far_column = across(row), ahead(column, STEPS[3])

time: 73.3 us -> 77.6 us (1.059)
  blocking collectives: 0 us -> 18.7 us
  starting transfers between devices: 34.2 us -> 22 us
  waiting for transfers between devices: 20.1 us -> 18.4 us
    all_to_all x0 -> x1, blocking collectives: none -> 18.7 us  [local(): lax.all_to_all(jnp.broadcast_to(wavefunction[None], (RUNS,) + wavefunctio...]
    all_to_all x1 -> x0, starting transfers between devices: 10.1 us -> none  [local(): lax.all_to_all(jnp.broadcast_to(wavefunction[None], (RUNS,) + wavefunctio...]
    all_to_all x1 -> x0, waiting for transfers between devices: 6.55 us -> none  [local(): lax.all_to_all(jnp.broadcast_to(wavefunction[None], (RUNS,) + wavefunctio...]
    ppermute x2, waiting for transfers between devices: 0.01 us -> 3.9 us  [across(): return lax.ppermute(value, 'y_hi', [(0, 1), (1, 0)])]
    ppermute x3, waiting for transfers between devices: 0.01 us -> 2.4 us  [ahead(): return lax.ppermute(value, 'x', [(x, (x + step) % 4) for x in range(4)])]
    ppermute x7, starting transfers between devices: 10.7 us -> 9.11 us  [swap_core(): return lax.ppermute(value, 'core', [(0, 1), (1, 0)])]
    ppermute x7, waiting for transfers between devices: 4.76 us -> 3.37 us  [swap_core(): return lax.ppermute(value, 'core', [(0, 1), (1, 0)])]
    all_to_all x1, starting transfers between devices: 5.66 us -> 4.83 us  [local(): summed = lax.all_to_all(half, ('y_lo', 'z'), 0, 0).sum(0)]
  transfers between devices with their start and end apart: 14 -> 13, of which waited for: 8 -> 7; matrix products, arithmetic and copies ran while one was open for 5% -> 5% of each run, Pallas kernels for 8% -> 7%
where the time goes in v5:
time: 77.6 us; the launch traced here: 76.2 us
  starting transfers between devices  22 us (28%)
  blocking collectives  18.7 us (24%)
  waiting for transfers between devices  18.4 us (24%)
  Pallas kernels  11 us (14%)
  other arithmetic  4.54 us (6%)
  local copies, waits for them, and re-layouts  1.5 us (2%)
    all_to_all x1, blocking collectives, local(): lax.all_to_all(jnp.broadcast_to(wavefunction[None], (RUNS,) + wavefunctio...  18.7 us
    pallas_call x2, Pallas kernels, chunk(): pl.pallas_call(kernel, in_specs=[smem] * 3 + [vmem] * len(arrays) + [hbm]...  11 us
    ppermute x7, starting transfers between devices, swap_core(): return lax.ppermute(value, 'core', [(0, 1), (1, 0)])  9.11 us
    all_to_all x1, waiting for transfers between devices, local(): summed = lax.all_to_all(half, ('y_lo', 'z'), 0, 0).sum(0)  8.78 us
    ppermute x3, starting transfers between devices, ahead(): return lax.ppermute(value, 'x', [(x, (x + step) % 4) for x in range(4)])  5.13 us
    all_to_all x1, starting transfers between devices, local(): summed = lax.all_to_all(half, ('y_lo', 'z'), 0, 0).sum(0)  4.83 us
    ppermute x2, waiting for transfers between devices, across(): return lax.ppermute(value, 'y_hi', [(0, 1), (1, 0)])  3.9 us
    ppermute x7, waiting for transfers between devices, swap_core(): return lax.ppermute(value, 'core', [(0, 1), (1, 0)])  3.37 us
  transfers between devices with their start and end apart: 13, of which 7 were waited for; matrix products, arithmetic and copies ran while one was open for 5% of the time, Pallas kernels for 7%

profile of v5, /device:TPU:1, one launch (start us, length us, event | category | flops | bytes accessed | tf_op | source)
XLA Modules:
  0.0 76.2 jit_solution(3715209180183635255)
XLA Ops:
  0.0 0.7 broadcast_in_dim.29
  0.7 18.7 %all_to_all.10 = f32[16,2,8,256]{3,2,1,0:T(8,128)S(1)} all-to-all(f32[16,2,8,256]{3,2,1,0:T(8,128)S(1)} %broadcast_in_dim.29), channel_id=1, replica_groups=mesh['y_hi'=2,'x'=4,'y_lo'=2,'z'=8,'core'=2] {'y_lo','z'}, dimensions={0} | all-to-all | bytes 524288 | tf_op jit(solution)/shard_map/all_to_all | solution.py:158
  19.4 2.6 %collective-permute-start = (f32[1,16,2,8,256]{4,3,2,1,0:T(8,128)S(1)}, f32[1,16,2,8,256]{4,3,2,1,0:T(8,128)S(1)}, u32[]{:S(2)}, u32[]{:S(2)}) collective-permute-start(f32[1,16,2,8,256]{4,3,2,1,0:T(8,128)S(1)} %bitcast.17), channel_id=1, source_target_pairs={{0,128},{128,0},{1,129},{129,1},{2,130},{130,2},{3,131},{131,3},{4... | collective-permute-start | bytes 786440 | tf_op jit(solution)/shard_map/ppermute | solution.py:148
  22.0 1.2 %collective-permute-start.1 = (f32[1,16,2,8,256]{4,3,2,1,0:T(8,128)S(1)}, f32[1,16,2,8,256]{4,3,2,1,0:T(8,128)S(1)}, u32[]{:S(2)}, u32[]{:S(2)}) collective-permute-start(f32[1,16,2,8,256]{4,3,2,1,0:T(8,128)S(1)} %bitcast.18), channel_id=1, source_target_pairs={{0,32},{32,64},{64,96},{96,0},{1,33},{33,65},{65,97},{97,1},{2,34}... | collective-permute-start | bytes 786440 | tf_op jit(solution)/shard_map/ppermute | solution.py:144
  23.2 1.5 %collective-permute-start.2 = (f32[1,16,2,8,256]{4,3,2,1,0:T(8,128)S(1)}, f32[1,16,2,8,256]{4,3,2,1,0:T(8,128)S(1)}, u32[]{:S(2)}, u32[]{:S(2)}) collective-permute-start(f32[1,16,2,8,256]{4,3,2,1,0:T(8,128)S(1)} %bitcast.19), channel_id=1, source_target_pairs={{0,96},{32,0},{64,32},{96,64},{1,97},{33,1},{65,33},{97,65},{2,98}... | collective-permute-start | bytes 786440 | tf_op jit(solution)/shard_map/ppermute | solution.py:144
  24.7 3.2 %collective-permute-start.5 = (f32[1,16,2,8,256]{4,3,2,1,0:T(8,128)S(1)}, f32[1,16,2,8,256]{4,3,2,1,0:T(8,128)S(1)}, u32[]{:S(2)}, u32[]{:S(2)}) collective-permute-start(f32[1,16,2,8,256]{4,3,2,1,0:T(8,128)S(1)} %bitcast.20), channel_id=1, source_target_pairs={{0,1},{1,0},{2,3},{3,2},{4,5},{5,4},{6,7},{7,6},{8,9},{9,8},{10,11... | collective-permute-start | bytes 786440 | tf_op jit(solution)/shard_map/ppermute | solution.py:140
  27.9 0.0 collective-permute-done.refs_5_
  27.9 0.9 %collective-permute-done.1.refs_7_ = f32[1,16,2,8,256]{4,3,2,1,0:T(8,128)S(1)} collective-permute-done((f32[1,16,2,8,256]{4,3,2,1,0:T(8,128)S(1)}, f32[1,16,2,8,256]{4,3,2,1,0:T(8,128)S(1)}, u32[]{:S(2)}, u32[]{:S(2)}) %collective-permute-start.1) | collective-permute-done | bytes 262176 | tf_op jit(solution)/shard_map/ppermute | solution.py:144
  28.8 0.0 collective-permute-done.2.refs_9_
  28.8 3.8 %collective-permute-start.7 = (f32[1,16,2,8,256]{4,3,2,1,0:T(8,128)S(1)}, f32[1,16,2,8,256]{4,3,2,1,0:T(8,128)S(1)}, u32[]{:S(2)}, u32[]{:S(2)}) collective-permute-start(f32[1,16,2,8,256]{4,3,2,1,0:T(8,128)S(1)} %collective-permute-done.1.refs_7_), channel_id=1, source_target_pairs={{0,1},{1,0},{2,3},{3,2},{4,5},{5,4},{6,7},{7,6},{8,9},{9,8},{10,11... | collective-permute-start | bytes 786440 | tf_op jit(solution)/shard_map/ppermute | solution.py:140
  32.5 0.0 collective-permute-start.8
  32.6 0.6 collective-permute-start.6
  33.2 0.7 copy.15
  33.9 0.3 collective-permute-start.3
  34.2 0.8 %select_reduce_fusion = f32[8,3]{0,1:T(4,128)S(1)} fusion(f32[26]{0:T(128)} %param.12, s32[8,3]{0,1:T(4,128)S(1)} %bitcast.27), kind=kLoop, calls=%fused_computation.3 | loop fusion | flops 1848 | bytes 296 | tf_op jit(solution)/shard_map/reduce_sum | solution.py:170
  35.0 0.7 fusion.refs_2_
  35.7 0.0 collective-permute-done.5.refs_4_
  35.7 2.5 %collective-permute-start.4 = (f32[2,16,2,8,256]{4,3,2,1,0:T(8,128)S(1)}, f32[2,16,2,8,256]{4,3,2,1,0:T(8,128)S(1)}, u32[]{:S(2)}, u32[]{:S(2)}) collective-permute-start(f32[2,16,2,8,256]{4,3,2,1,0:T(8,128)S(1)} %pad_maximum_fusion.1), channel_id=1, source_target_pairs={{0,64},{32,96},{64,0},{96,32},{1,65},{33,97},{65,1},{97,33},{2,66}... | collective-permute-start | bytes 1572872 | tf_op jit(solution)/shard_map/ppermute | solution.py:144
  38.2 0.7 minimum_bitcast_fusion.refs_0_
  38.9 0.7 add_bitcast_fusion.refs_1_
  39.6 0.0 collective-permute-done.6.refs_6_
  39.6 0.0 collective-permute-done.7.refs_8_
  39.6 0.0 collective-permute-done.8.refs_10_
  39.6 5.4 %shard_map.82.refs_9_ = f32[2,256,256]{2,1,0:T(8,128)S(1)} custom-call(s32[2,16]{1,0:T(2,128)S(1)} %minimum_bitcast_fusion.refs_0_, s32[1,3,1,8]{3,2,1,0:T(1,128)S(1)} %add_bitcast_fusion.refs_1_, f32[1,3,1,8]{3,2,1,0:T(1,128)S(1)} %fusion.refs_2_, f32[1,16,2,8,256]{4,3,2,1,0:T(8,128)S(1)} %bitcast.22, ...), custom_call_target="tpu_custom_call" | custom-call | flops 1000000000 | bytes 1048576 | tf_op jit(solution)/shard_map/pallas_call | solution.py:118
  45.0 3.9 %collective-permute-done.3.refs_3_ = f32[2,16,2,8,256]{4,3,2,1,0:T(8,128)S(1)} collective-permute-done((f32[2,16,2,8,256]{4,3,2,1,0:T(8,128)S(1)}, f32[2,16,2,8,256]{4,3,2,1,0:T(8,128)S(1)}, u32[]{:S(2)}, u32[]{:S(2)}) %collective-permute-start.3) | collective-permute-done | bytes 524320 | tf_op jit(solution)/shard_map/ppermute | solution.py:148
  48.9 1.5 %collective-permute-done.4.refs_5_ = f32[2,16,2,8,256]{4,3,2,1,0:T(8,128)S(1)} collective-permute-done((f32[2,16,2,8,256]{4,3,2,1,0:T(8,128)S(1)}, f32[2,16,2,8,256]{4,3,2,1,0:T(8,128)S(1)}, u32[]{:S(2)}, u32[]{:S(2)}) %collective-permute-start.4) | collective-permute-done | bytes 524320 | tf_op jit(solution)/shard_map/ppermute | solution.py:144
  50.4 1.1 %collective-permute-start.10 = (f32[2,16,2,8,256]{4,3,2,1,0:T(8,128)S(1)}, f32[2,16,2,8,256]{4,3,2,1,0:T(8,128)S(1)}, u32[]{:S(2)}, u32[]{:S(2)}) collective-permute-start(f32[2,16,2,8,256]{4,3,2,1,0:T(8,128)S(1)} %collective-permute-done.4.refs_5_), channel_id=1, source_target_pairs={{0,1},{1,0},{2,3},{3,2},{4,5},{5,4},{6,7},{7,6},{8,9},{9,8},{10,11... | collective-permute-start | bytes 1572872 | tf_op jit(solution)/shard_map/ppermute | solution.py:140
  51.6 0.0 collective-permute-start.9
  51.6 0.0 copy-start
  51.6 1.5 %collective-permute-done.10.refs_6_ = f32[2,16,2,8,256]{4,3,2,1,0:T(8,128)S(1)} collective-permute-done((f32[2,16,2,8,256]{4,3,2,1,0:T(8,128)S(1)}, f32[2,16,2,8,256]{4,3,2,1,0:T(8,128)S(1)}, u32[]{:S(2)}, u32[]{:S(2)}) %collective-permute-start.10) | collective-permute-done | bytes 524320 | tf_op jit(solution)/shard_map/ppermute | solution.py:140
  53.1 0.7 collective-permute-done.9.refs_4_
  53.9 5.5 %shard_map.83 = (f32[16,2,8,256]{3,2,1,0:T(8,128)S(1)}, f32[16,2,8,256]{3,2,1,0:T(8,128)S(1)}) custom-call(s32[2,16]{1,0:T(2,128)S(1)} %minimum_bitcast_fusion.refs_0_, s32[1,3,1,8]{3,2,1,0:T(1,128)S(1)} %add_bitcast_fusion.refs_1_, f32[1,3,1,8]{3,2,1,0:T(1,128)S(1)} %fusion.refs_2_, f32[2,16,2,8,256]{4,3,2,1,0:T(8,128)S(1)} %collective-permute-done.3.refs_3_, ...), custom_call_target="tpu_custom_call" | custom-call | flops 20000000000 | bytes 1048576 | tf_op jit(solution)/shard_map/pallas_call | solution.py:118
  59.4 0.5 collective-permute-start.11
  59.9 0.0 copy-done
  59.9 0.1 constant_dynamic-slice_fusion
  59.9 1.1 %collective-permute-done.11 = f32[16,2,8,256]{3,2,1,0:T(8,128)S(1)} collective-permute-done((f32[16,2,8,256]{3,2,1,0:T(8,128)S(1)}, f32[16,2,8,256]{3,2,1,0:T(8,128)S(1)}, u32[]{:S(2)}, u32[]{:S(2)}) %collective-permute-start.11) | collective-permute-done | bytes 262176 | tf_op jit(solution)/shard_map/ppermute | solution.py:140
  61.0 0.7 add.35
  61.8 4.8 %all-to-all-start.1 = ((f32[16,2,8,256]{3,2,1,0:T(8,128)}), f32[16,2,8,256]{3,2,1,0:T(8,128)S(1)}, u32[]{:S(2)}, u32[]{:S(2)}) async-start(f32[16,2,8,256]{3,2,1,0:T(8,128)} %add.35), calls=%async_computation.1 | async-start | bytes 524288 | tf_op jit(solution)/shard_map/all_to_all | solution.py:193
  66.6 0.1 iota_compare_fusion.1
  66.7 0.1 broadcast_compare_fusion
  66.8 8.8 %all-to-all-done.1 = f32[16,2,8,256]{3,2,1,0:T(8,128)S(1)} async-done(((f32[16,2,8,256]{3,2,1,0:T(8,128)}), f32[16,2,8,256]{3,2,1,0:T(8,128)S(1)}, u32[]{:S(2)}, u32[]{:S(2)}) %all-to-all-start.1) | async-done | bytes 262176 | tf_op jit(solution)/shard_map/all_to_all | solution.py:193
  75.6 0.7 and_select_fusion
  (5 shorter events, 0.1 us)
Async XLA Ops:
  19.4 8.5 %collective-permute-start = (f32[1,16,2,8,256]{4,3,2,1,0:T(8,128)S(1)}, f32[1,16,2,8,256]{4,3,2,1,0:T(8,128)S(1)}, u32[]{:S(2)}, u32[]{:S(2)}) collective-permute-start(f32[1,16,2,8,256]{4,3,2,1,0:T(8,128)S(1)} %bitcast.17), channel_id=1, source_target_pairs={{0,128},{128,0},{1,129},{129,1},{2,130},{130,2},{3,131},{131,3},{4... | collective-permute-start | bytes 786440 | tf_op jit(solution)/shard_map/ppermute | solution.py:148
  22.0 6.7 %collective-permute-start.1 = (f32[1,16,2,8,256]{4,3,2,1,0:T(8,128)S(1)}, f32[1,16,2,8,256]{4,3,2,1,0:T(8,128)S(1)}, u32[]{:S(2)}, u32[]{:S(2)}) collective-permute-start(f32[1,16,2,8,256]{4,3,2,1,0:T(8,128)S(1)} %bitcast.18), channel_id=1, source_target_pairs={{0,32},{32,64},{64,96},{96,0},{1,33},{33,65},{65,97},{97,1},{2,34}... | collective-permute-start | bytes 786440 | tf_op jit(solution)/shard_map/ppermute | solution.py:144
  23.2 5.5 %collective-permute-start.2 = (f32[1,16,2,8,256]{4,3,2,1,0:T(8,128)S(1)}, f32[1,16,2,8,256]{4,3,2,1,0:T(8,128)S(1)}, u32[]{:S(2)}, u32[]{:S(2)}) collective-permute-start(f32[1,16,2,8,256]{4,3,2,1,0:T(8,128)S(1)} %bitcast.19), channel_id=1, source_target_pairs={{0,96},{32,0},{64,32},{96,64},{1,97},{33,1},{65,33},{97,65},{2,98}... | collective-permute-start | bytes 786440 | tf_op jit(solution)/shard_map/ppermute | solution.py:144
  24.7 11.0 %collective-permute-start.5 = (f32[1,16,2,8,256]{4,3,2,1,0:T(8,128)S(1)}, f32[1,16,2,8,256]{4,3,2,1,0:T(8,128)S(1)}, u32[]{:S(2)}, u32[]{:S(2)}) collective-permute-start(f32[1,16,2,8,256]{4,3,2,1,0:T(8,128)S(1)} %bitcast.20), channel_id=1, source_target_pairs={{0,1},{1,0},{2,3},{3,2},{4,5},{5,4},{6,7},{7,6},{8,9},{9,8},{10,11... | collective-permute-start | bytes 786440 | tf_op jit(solution)/shard_map/ppermute | solution.py:140
  28.8 10.8 %collective-permute-start.7 = (f32[1,16,2,8,256]{4,3,2,1,0:T(8,128)S(1)}, f32[1,16,2,8,256]{4,3,2,1,0:T(8,128)S(1)}, u32[]{:S(2)}, u32[]{:S(2)}) collective-permute-start(f32[1,16,2,8,256]{4,3,2,1,0:T(8,128)S(1)} %collective-permute-done.1.refs_7_), channel_id=1, source_target_pairs={{0,1},{1,0},{2,3},{3,2},{4,5},{5,4},{6,7},{7,6},{8,9},{9,8},{10,11... | collective-permute-start | bytes 786440 | tf_op jit(solution)/shard_map/ppermute | solution.py:140
  32.5 7.1 %collective-permute-start.8 = (f32[1,16,2,8,256]{4,3,2,1,0:T(8,128)S(1)}, f32[1,16,2,8,256]{4,3,2,1,0:T(8,128)S(1)}, u32[]{:S(2)}, u32[]{:S(2)}) collective-permute-start(f32[1,16,2,8,256]{4,3,2,1,0:T(8,128)S(1)} %collective-permute-done.2.refs_9_), channel_id=1, source_target_pairs={{0,1},{1,0},{2,3},{3,2},{4,5},{5,4},{6,7},{7,6},{8,9},{9,8},{10,11... | collective-permute-start | bytes 786440 | tf_op jit(solution)/shard_map/ppermute | solution.py:140
  32.6 7.0 %collective-permute-start.6 = (f32[1,16,2,8,256]{4,3,2,1,0:T(8,128)S(1)}, f32[1,16,2,8,256]{4,3,2,1,0:T(8,128)S(1)}, u32[]{:S(2)}, u32[]{:S(2)}) collective-permute-start(f32[1,16,2,8,256]{4,3,2,1,0:T(8,128)S(1)} %collective-permute-done.refs_5_), channel_id=1, source_target_pairs={{0,1},{1,0},{2,3},{3,2},{4,5},{5,4},{6,7},{7,6},{8,9},{9,8},{10,11... | collective-permute-start | bytes 786440 | tf_op jit(solution)/shard_map/ppermute | solution.py:140
  33.9 15.0 %collective-permute-start.3 = (f32[2,16,2,8,256]{4,3,2,1,0:T(8,128)S(1)}, f32[2,16,2,8,256]{4,3,2,1,0:T(8,128)S(1)}, u32[]{:S(2)}, u32[]{:S(2)}) collective-permute-start(f32[2,16,2,8,256]{4,3,2,1,0:T(8,128)S(1)} %pad_maximum_fusion), channel_id=1, source_target_pairs={{0,128},{128,0},{1,129},{129,1},{2,130},{130,2},{3,131},{131,3},{4... | collective-permute-start | bytes 1572872 | tf_op jit(solution)/shard_map/ppermute | solution.py:148
  35.7 14.7 %collective-permute-start.4 = (f32[2,16,2,8,256]{4,3,2,1,0:T(8,128)S(1)}, f32[2,16,2,8,256]{4,3,2,1,0:T(8,128)S(1)}, u32[]{:S(2)}, u32[]{:S(2)}) collective-permute-start(f32[2,16,2,8,256]{4,3,2,1,0:T(8,128)S(1)} %pad_maximum_fusion.1), channel_id=1, source_target_pairs={{0,64},{32,96},{64,0},{96,32},{1,65},{33,97},{65,1},{97,33},{2,66}... | collective-permute-start | bytes 1572872 | tf_op jit(solution)/shard_map/ppermute | solution.py:144
  50.4 2.7 %collective-permute-start.10 = (f32[2,16,2,8,256]{4,3,2,1,0:T(8,128)S(1)}, f32[2,16,2,8,256]{4,3,2,1,0:T(8,128)S(1)}, u32[]{:S(2)}, u32[]{:S(2)}) collective-permute-start(f32[2,16,2,8,256]{4,3,2,1,0:T(8,128)S(1)} %collective-permute-done.4.refs_5_), channel_id=1, source_target_pairs={{0,1},{1,0},{2,3},{3,2},{4,5},{5,4},{6,7},{7,6},{8,9},{9,8},{10,11... | collective-permute-start | bytes 1572872 | tf_op jit(solution)/shard_map/ppermute | solution.py:140
  51.6 2.3 %collective-permute-start.9 = (f32[2,16,2,8,256]{4,3,2,1,0:T(8,128)S(1)}, f32[2,16,2,8,256]{4,3,2,1,0:T(8,128)S(1)}, u32[]{:S(2)}, u32[]{:S(2)}) collective-permute-start(f32[2,16,2,8,256]{4,3,2,1,0:T(8,128)S(1)} %collective-permute-done.3.refs_3_), channel_id=1, source_target_pairs={{0,1},{1,0},{2,3},{3,2},{4,5},{5,4},{6,7},{7,6},{8,9},{9,8},{10,11... | collective-permute-start | bytes 1572872 | tf_op jit(solution)/shard_map/ppermute | solution.py:140
  51.6 8.3 %copy-start = (s32[16,2]{0,1:T(2,128)S(1)}, s32[16,2]{0,1:T(2,128)}, u32[]{:S(2)}) copy-start(s32[16,2]{0,1:T(2,128)} %param.9) | copy-start | bytes 388
  59.4 1.6 %collective-permute-start.11 = (f32[16,2,8,256]{3,2,1,0:T(8,128)S(1)}, f32[16,2,8,256]{3,2,1,0:T(8,128)S(1)}, u32[]{:S(2)}, u32[]{:S(2)}) collective-permute-start(f32[16,2,8,256]{3,2,1,0:T(8,128)S(1)} %get-tuple-element.28), channel_id=1, source_target_pairs={{0,1},{1,0},{2,3},{3,2},{4,5},{5,4},{6,7},{7,6},{8,9},{9,8},{10,11... | collective-permute-start | bytes 786440 | tf_op jit(solution)/shard_map/ppermute | solution.py:140
  61.8 13.8 %all-to-all-start.1 = ((f32[16,2,8,256]{3,2,1,0:T(8,128)}), f32[16,2,8,256]{3,2,1,0:T(8,128)S(1)}, u32[]{:S(2)}, u32[]{:S(2)}) async-start(f32[16,2,8,256]{3,2,1,0:T(8,128)} %add.35), calls=%async_computation.1 | async-start | bytes 524288 | tf_op jit(solution)/shard_map/all_to_all | solution.py:193
